TPU v7x, 128 devices: a whole 4x4x4 slice. The times are simulated.
128 devices in a mesh: section: 4 (over z_hi, core), ctx: 32 (over z_lo, x, y).
Axes of the slice: x: 4, y: 4, z: 4 (z_hi: 2, z_lo: 2; z = z_hi * 2 + z_lo), core: 2. Of those that a mesh axis runs over, the one named last changes fastest.
Arguments:
- queries: bfloat16 [4, 16384, 1024], P('section', 'ctx'), may hold values from -6 to 6
- keys: bfloat16 [4, 16384, 128], P('section', 'ctx'), may hold values from -6 to 6
- values: bfloat16 [4, 16384, 128], P('section', 'ctx'), may hold values from -6 to 6
- outputs: bfloat16 [4, 16384, 1024], P('section', 'ctx'), may hold values from -6 to 6
- out_grads: bfloat16 [4, 16384, 1024], P('section', 'ctx'), may hold values from -12 to 12
- lse: float32 [4, 16384, 8], P('section', 'ctx')
- doc_start: int32 [4, 16384], P('section', 'ctx'), may hold values from 0 to 16383, as said below
Outputs:
- query_grads: bfloat16 [4, 16384, 1024], P('section', 'ctx')
- key_grads: bfloat16 [4, 16384, 128], P('section', 'ctx')
- value_grads: bfloat16 [4, 16384, 128], P('section', 'ctx')
Inputs may be any that keep to these rules, and one draw needn't show every extreme that they name: Per section, documents are contiguous: doc_start never falls, doc_start[i] <= i, and each document has 1 to 3584 tokens; the first document has exactly 3584.
All inputs are finite; a program needn't handle non-finite values.
Results may differ from a plain program's by a relative error of at most 0.0055.
Values may be sent and summed in bfloat16 or wider, within the bound.
No kernel may reach another device: no remote copies, remote signals or barrier semaphores. Data moves between devices by JAX's collectives and lax.ppermute only.
A program may use at most 128 MiB of HBM per device.

v0:
```python
import math

import jax
import jax.numpy as jnp
from jax import lax
from jax.experimental import pallas as pl
from jax.experimental.pallas import tpu as pltpu
from jax.sharding import PartitionSpec as P

HEADS = 8
HD = 128
ROWS = 512
HALF = 256
SCALE = HD**-0.5
LOG2E = math.log2(math.e)
F32 = jnp.float32
BF16 = jnp.bfloat16
LSE, DELTA, LSE_BACK = 0, HEADS, 2 * HEADS
WIDE = jax.ShapeDtypeStruct((HEADS * HD, ROWS), F32)
PAIR = jax.ShapeDtypeStruct((ROWS, 2 * HD), F32)


def dot(a, b, da, db):
    return lax.dot_general(a, b, (((da,), (db,)), ((), ())), preferred_element_type=F32)


def lanes(h):
    return pl.ds(pl.multiple_of(h * HD, HD), HD)


def terms(refs, h, to_h, lse_at, keys_at, n_keys, rows, ok):
    q_ref, do_ref, ld_ref, kv_ref, kt_ref, dq_ref, dk_ref, dv_ref = refs
    here = pl.ds(keys_at, n_keys)
    q = q_ref[rows, lanes(h)]
    do = do_ref[rows, lanes(h)]
    x = dot(kv_ref[here, :HD], q, 1, 1) * (SCALE * LOG2E) - ld_ref[pl.ds(lse_at + h, 1), rows]
    p = jnp.exp2(x)
    if ok is not None:
        p = jnp.where(ok, p, 0.0)
    dp = dot(kv_ref[here, HD:], do, 1, 1) - ld_ref[pl.ds(DELTA + h, 1), rows]
    ds = (p * dp).astype(BF16)
    dv_ref[here, :] += dot(p.astype(BF16), do, 1, 0)
    dk_ref[here, :] += dot(ds, q, 1, 0)
    dq_ref[lanes(to_h), rows] += dot(kt_ref[:, here], ds, 1, 0)


def finish(dq_ref, q_out):
    for h in range(q_out.shape[1] // HD):
        cols = slice(h * HD, (h + 1) * HD)
        q_out[:, cols] = (dq_ref[cols, :] * SCALE).astype(BF16).T


def own_terms(first, n, to, start_row, base, refs):
    kv_ref, kt_ref = refs[3], refs[4]
    kt_ref[...] = kv_ref[:, :HD].T

    def head(h, carry):
        for at, rows in ((0, slice(0, ROWS)), (HALF, slice(HALF, ROWS))):
            n_rows = rows.stop - rows.start
            key = lax.broadcasted_iota(jnp.int32, (HALF, n_rows), 0)
            ok = key >= start_row[:, rows] - (base + at)
            ok = ok & (key + (at - rows.start) <= lax.broadcasted_iota(jnp.int32, (HALF, n_rows), 1))
            terms(refs, h, h - to, LSE, at, HALF, rows, ok)
        return carry

    lax.fori_loop(first, first + n, head, 0)


def first_kernel(n, base_ref, starts, start_row, q_ref, do_ref, o_ref, lse_ref, kv_ref, dq_ref, ld_ref, out_ref, kt_ref, dk_ref, dv_ref):
    lse = lse_ref[...] * LOG2E
    ld_ref[LSE : LSE + HEADS, :] = lse
    ld_ref[LSE_BACK : LSE_BACK + HEADS, :] = jnp.where(start_row[...] == starts[0, 0], lse, 1e30)
    ones = jnp.ones((8, HD), BF16)
    for h in range(HEADS):
        cols = slice(h * HD, (h + 1) * HD)
        x = do_ref[:, cols].astype(F32) * o_ref[:, cols].astype(F32)
        hi = x.astype(BF16)
        lo = (x - hi.astype(F32)).astype(BF16)
        row = dot(ones, hi, 1, 1) + dot(ones, lo, 1, 1)
        ld_ref[DELTA + h : DELTA + h + 1, :] = row[:1]
    dq_ref[...] = jnp.zeros_like(dq_ref)
    dk_ref[...] = jnp.zeros_like(dk_ref)
    dv_ref[...] = jnp.zeros_like(dv_ref)
    own_terms(0, n, 0, start_row, base_ref[0], (q_ref, do_ref, ld_ref, kv_ref, kt_ref, dq_ref, dk_ref, dv_ref))
    out_ref[:, :HD] = dk_ref[...]
    out_ref[:, HD:] = dv_ref[...]


def final_kernel(first, n, base_ref, starts, start_row, q_ref, do_ref, ld_ref, kv_ref, dq_in, sum_in, *rest):
    q_out, out_ref, dq_ref, kt_ref, dk_ref, dv_ref = rest[-6:]
    dq_ref[...] = dq_in[first * HD : (first + n) * HD, :]
    dk_ref[...] = sum_in[:, :HD]
    dv_ref[...] = sum_in[:, HD:]
    own_terms(first, n, first, start_row, base_ref[0], (q_ref, do_ref, ld_ref, kv_ref, kt_ref, dq_ref, dk_ref, dv_ref))
    finish(dq_ref, q_out)
    out_ref[:, :HD] = dk_ref[...] * SCALE
    out_ref[:, HD:] = dv_ref[...]


def back_kernel(ds, first, n, emit, has_sum, sum_out, extra, base_ref, starts, start_row, q_ref, do_ref, ld_ref, dq_in, *rest):
    m = len(ds)
    kv_refs, rest = rest[:m], rest[m:]
    sum_in = rest[0] if has_sum else None
    rest = rest[has_sum + extra :]
    head_out, out_refs, rest = rest[0], rest[1 : m + 1], rest[m + 1 :]
    kv_ref, kt_ref, dk_ref, dv_ref, *rest = rest
    base, start = base_ref[0], starts[0, 0]
    if emit:
        dq_ref, to = rest[0], first
        dq_ref[...] = dq_in[first * HD : (first + n) * HD, :]
    else:
        dq_ref, to = head_out, 0
    if has_sum:
        dk_ref[...] = sum_in[:, :HD]
        dv_ref[...] = sum_in[:, HD:]
    else:
        dk_ref[...] = jnp.zeros_like(dk_ref)
        dv_ref[...] = jnp.zeros_like(dv_ref)
    reach = lax.shift_right_logical(base - start + (ROWS - 1), 9)
    skipped = jnp.clip(ds[0] - reach, 0, m)
    refs = (q_ref, do_ref, ld_ref, kv_ref, kt_ref, dq_ref, dk_ref, dv_ref)

    def seen(d, width):
        key = lax.broadcasted_iota(jnp.int32, (ROWS, width), 0)
        return key >= start - (base - d * ROWS)

    @pl.when(skipped < m)
    def _():
        for b, d in enumerate(ds):
            here = slice(b * ROWS, (b + 1) * ROWS)
            kv = kv_refs[b][...].astype(F32)
            kv_ref[here, :] = jnp.where(seen(d, 2 * HD), kv, kv[ROWS - 1 :, :]).astype(BF16)
            kt_ref[:, here] = jnp.where(seen(d, HD), kv[:, :HD], 0.0).astype(BF16).T

        def step(w, carry):
            w = w * 2
            keys_at = pl.multiple_of((skipped + w // n) * ROWS, ROWS)
            for h in (first + w % n, first + w % n + 1):
                terms(refs, h, h - to, LSE_BACK, keys_at, ROWS, slice(0, ROWS), None)
            return carry

        lax.fori_loop(0, (m - skipped) * (n // 2), step, 0)

    for b, d in enumerate(ds):
        here = slice(b * ROWS, (b + 1) * ROWS)
        if sum_out:
            out_refs[b][:, :HD] = dk_ref[here, :]
            out_refs[b][:, HD:] = dv_ref[here, :]
        else:
            ok = seen(d, HD)
            out_refs[b][:, :HD] = jnp.where(ok, dk_ref[here, :] * SCALE, 0.0).astype(BF16)
            out_refs[b][:, HD:] = jnp.where(ok, dv_ref[here, :], 0.0).astype(BF16)
    if emit:
        finish(dq_ref, head_out)


def work(pairs):
    flops = int(pairs * 5 * 2 * ROWS * ROWS * HD * HEADS)
    return pl.CostEstimate(flops=flops, bytes_accessed=1 << 20, transcendentals=0)


def scratch(m):
    return [pltpu.VMEM((HD, m * ROWS), BF16), pltpu.VMEM((m * ROWS, HD), F32), pltpu.VMEM((m * ROWS, HD), F32)]


def call(kernel, name, pairs, operands, outs, scratch_shapes, extra=(), aliases=None):
    return pl.pallas_call(
        kernel,
        out_shape=outs,
        in_specs=[pl.BlockSpec(memory_space=pltpu.SMEM)] * 2
        + [pl.BlockSpec(memory_space=pltpu.VMEM)] * (len(operands) - 2)
        + [pl.BlockSpec(memory_space=pl.ANY)] * len(extra),
        out_specs=[pl.BlockSpec(memory_space=pltpu.VMEM)] * len(outs),
        input_output_aliases=aliases or {},
        scratch_shapes=scratch_shapes,
        compiler_params=pltpu.CompilerParams(vmem_limit_bytes=24 << 20),
        cost_estimate=work(pairs),
        name=name,
    )(*operands, *extra)


def shifted(block, axis, distance):
    devices = range(lax.axis_size(axis))
    route = [((i - distance) % len(devices), i) for i in devices]
    return lax.ppermute(block, axis, route)


def per_device(queries, keys, values, outputs, out_grads, lse, doc_start):
    q, do, o = queries[0], out_grads[0], outputs[0]
    base = (lax.axis_index("ctx") * ROWS).astype(jnp.int32)[None]
    common = (base, doc_start, doc_start, q, do)
    kv = jnp.concatenate([keys[0], values[0]], axis=1)
    held = {d: shifted(kv, "ctx", d) for d in (6, 7, 5, 4, 3, 2, 1)}
    part = jax.ShapeDtypeStruct((ROWS, 2 * HD), BF16)
    split = HEADS // 2
    half = jax.ShapeDtypeStruct((ROWS, split * HD), BF16)
    stats = jax.ShapeDtypeStruct((3 * HEADS, ROWS), F32)
    own_scratch = scratch(1)

    def first(*refs):
        first_kernel(split, *refs)

    dq, ld, own = call(first, "own_first", 0.4, (*common, o, lse[0].T, kv), [WIDE, stats, PAIR], own_scratch)

    def back(ds, dq, first=0, n=HEADS, emit=False, sum_in=None, sum_out=False, extra=()):
        m = len(ds)
        sums = () if sum_in is None else (sum_in,)

        def kernel(*refs):
            back_kernel(ds, first, n, emit, len(sums), sum_out, len(extra), *refs)

        head = jax.ShapeDtypeStruct((ROWS, n * HD), BF16) if emit else WIDE
        last = [pltpu.VMEM((n * HD, ROWS), F32)] if emit else []
        return call(
            kernel,
            "back_%s_%d" % ("_".join(map(str, ds)), first),
            m * n / HEADS,
            (*common, ld, dq, *[held[d] for d in ds], *sums),
            [head] + [PAIR if sum_out else part] * m,
            [pltpu.VMEM((m * ROWS, 2 * HD), BF16)] + scratch(m) + last,
            extra,
            {} if emit else {6: 0},
        )

    got = {}

    def give_back(ds, outs):
        for d, out in zip(ds, outs):
            got[d] = shifted(out, "ctx", -d)

    dq, *outs = back((7, 6), dq)
    give_back((7, 6), outs)
    dq, *outs = back((5, 4), dq)
    give_back((5, 4), outs)
    dq, *outs = back((3, 2), dq, extra=(got[7], got[6]))
    give_back((3, 2), outs)
    q_a, sum_1 = back((1,), dq, 0, split, True, None, True)
    handed_a = shifted(q_a, "section", -1)
    dq, out = back((1,), dq, split, split, False, sum_1, False, (got[5], got[4]))
    give_back((1,), [out])

    def final(*refs):
        final_kernel(split, split, *refs)

    q_b, own = call(
        final, "own_last", 0.4, (*common, ld, kv, dq, own), [half, PAIR],
        [pltpu.VMEM((split * HD, ROWS), F32)] + own_scratch, (got[3], got[2]),
    )
    handed_b = shifted(q_b, "section", -1)
    total = own
    for d in (7, 6, 5, 4, 3, 2, 1):
        total = total + got[d].astype(F32)
    kv_g = shifted(total.astype(BF16), "section", -1)
    return (jnp.concatenate([handed_a, handed_b], axis=1)[None], kv_g[None, :, :HD], kv_g[None, :, HD:])


def solution(mesh):
    wide = P("section", "ctx", None)
    in_specs = (wide, wide, wide, wide, wide, wide, P("section", "ctx"))
    return jax.shard_map(per_device, mesh=mesh, in_specs=in_specs, out_specs=(wide, wide, wide), check_vma=False)
```

profile of v0, /device:TPU:31, one launch (start us, length us, event | category | flops | bytes accessed | tf_op | source)
XLA Modules:
  0.0 128.3 jit_solution(12354721358363625996)
XLA Ops:
  0.6 1.0 pad_maximum_fusion.refs_7_.refs_6_
  1.6 3.2 %collective-permute-start.1 = (bf16[512,256]{1,0:T(8,128)(2,1)S(1)}, bf16[512,256]{1,0:T(8,128)(2,1)S(1)}, u32[]{:S(2)}, u32[]{:S(2)}) collective-permute-start(bf16[512,256]{1,0:T(8,128)(2,1)S(1)} %pad_maximum_fusion.refs_7_.refs_6_), channel_id=1, source_target_pairs={{26,0},{27,1},{28,2},{29,3},{30,4},{31,5},{0,6},{1,7},{2,8},{3,9},... | collective-permute-start | bytes 786440 | tf_op jit(solution)/shard_map/ppermute | solution.py:185
  4.9 1.1 collective-permute-start
  6.0 3.1 %collective-permute-start.8 = (bf16[512,256]{1,0:T(8,128)(2,1)S(1)}, bf16[512,256]{1,0:T(8,128)(2,1)S(1)}, u32[]{:S(2)}, u32[]{:S(2)}) collective-permute-start(bf16[512,256]{1,0:T(8,128)(2,1)S(1)} %pad_maximum_fusion.refs_7_.refs_6_), channel_id=1, source_target_pairs={{31,0},{0,1},{1,2},{2,3},{3,4},{4,5},{5,6},{6,7},{7,8},{8,9},{9,10... | collective-permute-start | bytes 786440 | tf_op jit(solution)/shard_map/ppermute | solution.py:185
  9.1 1.4 %collective-permute-start.5 = (bf16[512,256]{1,0:T(8,128)(2,1)S(1)}, bf16[512,256]{1,0:T(8,128)(2,1)S(1)}, u32[]{:S(2)}, u32[]{:S(2)}) collective-permute-start(bf16[512,256]{1,0:T(8,128)(2,1)S(1)} %pad_maximum_fusion.refs_7_.refs_6_), channel_id=1, source_target_pairs={{30,0},{31,1},{0,2},{1,3},{2,4},{3,5},{4,6},{5,7},{6,8},{7,9},{8,1... | collective-permute-start | bytes 786440 | tf_op jit(solution)/shard_map/ppermute | solution.py:185
  10.5 1.2 copy-done
  11.7 1.2 copy-done.1
  13.6 1.2 copy-done.3
  15.6 4.8 %own_first.1 = (f32[1024,512]{1,0:T(8,128)S(1)}, f32[24,512]{1,0:T(8,128)S(1)}, f32[512,256]{1,0:T(8,128)S(1)}) custom-call(s32[1]{0:T(128)} %bitcast.refs_0_, s32[1,512]{1,0:T(1,128)S(1)} %copy-done.2, s32[1,512]{1,0:T(1,128)S(1)} %copy-done.2, bf16[512,1024]{1,0:T(8,128)(2,1)S(1)} %bitcast.15, bf16[512,1024]{1,0:T(8,128)(2,1)S(1)} %bitcast.22, ...), custom_call_target="tpu_custom_call" | custom-call | flops 1073741824 | bytes 1048576 | tf_op jit(solution)/shard_map/own_first/pallas_call | solution.py:167
  20.5 3.6 %collective-permute-start.2 = (bf16[512,256]{1,0:T(8,128)(2,1)S(1)}, bf16[512,256]{1,0:T(8,128)(2,1)S(1)}, u32[]{:S(2)}, u32[]{:S(2)}) collective-permute-start(bf16[512,256]{1,0:T(8,128)(2,1)S(1)} %pad_maximum_fusion.refs_7_.refs_6_), channel_id=1, source_target_pairs={{27,0},{28,1},{29,2},{30,3},{31,4},{0,5},{1,6},{2,7},{3,8},{4,9},{... | collective-permute-start | bytes 786440 | tf_op jit(solution)/shard_map/ppermute | solution.py:185
  24.9 28.4 %collective-permute-done.3.refs_8_ = bf16[512,256]{1,0:T(8,128)(2,1)S(1)} collective-permute-done((bf16[512,256]{1,0:T(8,128)(2,1)S(1)}, bf16[512,256]{1,0:T(8,128)(2,1)S(1)}, u32[]{:S(2)}, u32[]{:S(2)}) %collective-permute-start.3) | collective-permute-done | bytes 262176 | tf_op jit(solution)/shard_map/ppermute | solution.py:185
  54.1 7.2 %collective-permute-start.10 = (bf16[512,256]{1,0:T(8,128)(2,1)S(1)}, bf16[512,256]{1,0:T(8,128)(2,1)S(1)}, u32[]{:S(2)}, u32[]{:S(2)}) collective-permute-start(bf16[512,256]{1,0:T(8,128)(2,1)S(1)} %get-tuple-element.30), channel_id=1, source_target_pairs={{5,0},{6,1},{7,2},{8,3},{9,4},{10,5},{11,6},{12,7},{13,8},{14,9},{... | collective-permute-start | bytes 786440 | tf_op jit(solution)/shard_map/ppermute | solution.py:185
  61.3 10.1 %collective-permute-start.11 = (bf16[512,256]{1,0:T(8,128)(2,1)S(1)}, bf16[512,256]{1,0:T(8,128)(2,1)S(1)}, u32[]{:S(2)}, u32[]{:S(2)}) collective-permute-start(bf16[512,256]{1,0:T(8,128)(2,1)S(1)} %get-tuple-element.31), channel_id=1, source_target_pairs={{4,0},{5,1},{6,2},{7,3},{8,4},{9,5},{10,6},{11,7},{12,8},{13,9},{1... | collective-permute-start | bytes 786440 | tf_op jit(solution)/shard_map/ppermute | solution.py:185
  71.5 1.7 %collective-permute-done.7.refs_10_ = bf16[512,256]{1,0:T(8,128)(2,1)S(1)} collective-permute-done((bf16[512,256]{1,0:T(8,128)(2,1)S(1)}, bf16[512,256]{1,0:T(8,128)(2,1)S(1)}, u32[]{:S(2)}, u32[]{:S(2)}) %collective-permute-start.7) | collective-permute-done | bytes 262176 | tf_op jit(solution)/shard_map/ppermute | solution.py:185
  74.0 12.7 %collective-permute-start.12 = (bf16[512,256]{1,0:T(8,128)(2,1)S(1)}, bf16[512,256]{1,0:T(8,128)(2,1)S(1)}, u32[]{:S(2)}, u32[]{:S(2)}) collective-permute-start(bf16[512,256]{1,0:T(8,128)(2,1)S(1)} %get-tuple-element.34), channel_id=1, source_target_pairs={{3,0},{4,1},{5,2},{6,3},{7,4},{8,5},{9,6},{10,7},{11,8},{12,9},{13... | collective-permute-start | bytes 786440 | tf_op jit(solution)/shard_map/ppermute | solution.py:185
  86.6 4.0 %back_1_0.1 = (bf16[512,512]{1,0:T(8,128)(2,1)S(1)}, f32[512,256]{1,0:T(8,128)S(1)}) custom-call(s32[1]{0:T(128)} %bitcast.refs_0_, s32[1,512]{1,0:T(1,128)S(1)} %copy-done.2, s32[1,512]{1,0:T(1,128)S(1)} %copy-done.2, bf16[512,1024]{1,0:T(8,128)(2,1)S(1)} %bitcast.19, bf16[512,1024]{1,0:T(8,128)(2,1)S(1)} %bitcast.26, ...), custom_call_target="tpu_custom_call" | custom-call | flops 1342177280 | bytes 1048576 | tf_op jit(solution)/shard_map/back_1_0/pallas_call | solution.py:167
  90.6 3.6 %back_1_4.1 = (f32[1024,512]{1,0:T(8,128)S(1)}, bf16[512,256]{1,0:T(8,128)(2,1)S(1)}) custom-call(s32[1]{0:T(128)} %bitcast.refs_0_, s32[1,512]{1,0:T(1,128)S(1)} %copy-done.2, s32[1,512]{1,0:T(1,128)S(1)} %copy-done.2, bf16[512,1024]{1,0:T(8,128)(2,1)S(1)} %bitcast.20, bf16[512,1024]{1,0:T(8,128)(2,1)S(1)} %bitcast.27, ...), custom_call_target="tpu_custom_call", output_to_operand_aliasing={{0}: (6, {})} | custom-call | flops 1342177280 | bytes 1048576 | tf_op jit(solution)/shard_map/back_1_4/pallas_call | solution.py:167
  95.0 2.7 %collective-permute-start.9 = (bf16[512,512]{1,0:T(8,128)(2,1)S(1)}, bf16[512,512]{1,0:T(8,128)(2,1)S(1)}, u32[]{:S(2)}, u32[]{:S(2)}) collective-permute-start(bf16[512,512]{1,0:T(8,128)(2,1)S(1)} %get-tuple-element.28), channel_id=1, source_target_pairs={{32,0},{64,32},{96,64},{0,96},{33,1},{65,33},{97,65},{1,97},{34,2}... | collective-permute-start | bytes 1572872 | tf_op jit(solution)/shard_map/ppermute | solution.py:185
  97.9 2.2 %collective-permute-done.13.refs_10_ = bf16[512,256]{1,0:T(8,128)(2,1)S(1)} collective-permute-done((bf16[512,256]{1,0:T(8,128)(2,1)S(1)}, bf16[512,256]{1,0:T(8,128)(2,1)S(1)}, u32[]{:S(2)}, u32[]{:S(2)}) %collective-permute-start.13) | collective-permute-done | bytes 262176 | tf_op jit(solution)/shard_map/ppermute | solution.py:185
  100.1 4.3 %own_last.1 = (bf16[512,512]{1,0:T(8,128)(2,1)S(1)}, f32[512,256]{1,0:T(8,128)S(1)}) custom-call(s32[1]{0:T(128)} %bitcast.refs_0_, s32[1,512]{1,0:T(1,128)S(1)} %copy-done.2, s32[1,512]{1,0:T(1,128)S(1)} %copy-done.2, bf16[512,1024]{1,0:T(8,128)(2,1)S(1)} %bitcast.21, bf16[512,1024]{1,0:T(8,128)(2,1)S(1)} %bitcast.28, ...), custom_call_target="tpu_custom_call" | custom-call | flops 1073741824 | bytes 1048576 | tf_op jit(solution)/shard_map/own_last/pallas_call | solution.py:167
  104.4 2.7 %collective-permute-start.14 = (bf16[512,512]{1,0:T(8,128)(2,1)S(1)}, bf16[512,512]{1,0:T(8,128)(2,1)S(1)}, u32[]{:S(2)}, u32[]{:S(2)}) collective-permute-start(bf16[512,512]{1,0:T(8,128)(2,1)S(1)} %get-tuple-element.36), channel_id=1, source_target_pairs={{32,0},{64,32},{96,64},{0,96},{33,1},{65,33},{97,65},{1,97},{34,2}... | collective-permute-start | bytes 1572872 | tf_op jit(solution)/shard_map/ppermute | solution.py:185
  107.3 1.4 %collective-permute-start.16 = (bf16[512,256]{1,0:T(8,128)(2,1)S(1)}, bf16[512,256]{1,0:T(8,128)(2,1)S(1)}, u32[]{:S(2)}, u32[]{:S(2)}) collective-permute-start(bf16[512,256]{1,0:T(8,128)(2,1)S(1)} %add_convert_fusion), channel_id=1, source_target_pairs={{32,0},{64,32},{96,64},{0,96},{33,1},{65,33},{97,65},{1,97},{34,2}... | collective-permute-start | bytes 786440 | tf_op jit(solution)/shard_map/ppermute | solution.py:185
  108.7 17.8 %collective-permute-done.16 = bf16[512,256]{1,0:T(8,128)(2,1)S(1)} collective-permute-done((bf16[512,256]{1,0:T(8,128)(2,1)S(1)}, bf16[512,256]{1,0:T(8,128)(2,1)S(1)}, u32[]{:S(2)}, u32[]{:S(2)}) %collective-permute-start.16) | collective-permute-done | bytes 262176 | tf_op jit(solution)/shard_map/ppermute | solution.py:185
  127.2 1.1 maximum_bitcast_fusion
  (31 shorter events, 5.8 us)
Async XLA Ops:
  1.6 18.7 %collective-permute-start.1 = (bf16[512,256]{1,0:T(8,128)(2,1)S(1)}, bf16[512,256]{1,0:T(8,128)(2,1)S(1)}, u32[]{:S(2)}, u32[]{:S(2)}) collective-permute-start(bf16[512,256]{1,0:T(8,128)(2,1)S(1)} %pad_maximum_fusion.refs_7_.refs_6_), channel_id=1, source_target_pairs={{26,0},{27,1},{28,2},{29,3},{30,4},{31,5},{0,6},{1,7},{2,8},{3,9},... | collective-permute-start | bytes 786440 | tf_op jit(solution)/shard_map/ppermute | solution.py:185
  4.9 15.6 %collective-permute-start = (bf16[512,256]{1,0:T(8,128)(2,1)S(1)}, bf16[512,256]{1,0:T(8,128)(2,1)S(1)}, u32[]{:S(2)}, u32[]{:S(2)}) collective-permute-start(bf16[512,256]{1,0:T(8,128)(2,1)S(1)} %pad_maximum_fusion.refs_7_.refs_6_), channel_id=1, source_target_pairs={{25,0},{26,1},{27,2},{28,3},{29,4},{30,5},{31,6},{0,7},{1,8},{2,9}... | collective-permute-start | bytes 786440 | tf_op jit(solution)/shard_map/ppermute | solution.py:185
  6.0 80.7 %collective-permute-start.8 = (bf16[512,256]{1,0:T(8,128)(2,1)S(1)}, bf16[512,256]{1,0:T(8,128)(2,1)S(1)}, u32[]{:S(2)}, u32[]{:S(2)}) collective-permute-start(bf16[512,256]{1,0:T(8,128)(2,1)S(1)} %pad_maximum_fusion.refs_7_.refs_6_), channel_id=1, source_target_pairs={{31,0},{0,1},{1,2},{2,3},{3,4},{4,5},{5,6},{6,7},{7,8},{8,9},{9,10... | collective-permute-start | bytes 786440 | tf_op jit(solution)/shard_map/ppermute | solution.py:185
  9.1 45.0 %collective-permute-start.5 = (bf16[512,256]{1,0:T(8,128)(2,1)S(1)}, bf16[512,256]{1,0:T(8,128)(2,1)S(1)}, u32[]{:S(2)}, u32[]{:S(2)}) collective-permute-start(bf16[512,256]{1,0:T(8,128)(2,1)S(1)} %pad_maximum_fusion.refs_7_.refs_6_), channel_id=1, source_target_pairs={{30,0},{31,1},{0,2},{1,3},{2,4},{3,5},{4,6},{5,7},{6,8},{7,9},{8,1... | collective-permute-start | bytes 786440 | tf_op jit(solution)/shard_map/ppermute | solution.py:185
  10.5 50.8 %collective-permute-start.4 = (bf16[512,256]{1,0:T(8,128)(2,1)S(1)}, bf16[512,256]{1,0:T(8,128)(2,1)S(1)}, u32[]{:S(2)}, u32[]{:S(2)}) collective-permute-start(bf16[512,256]{1,0:T(8,128)(2,1)S(1)} %pad_maximum_fusion.refs_7_.refs_6_), channel_id=1, source_target_pairs={{29,0},{30,1},{31,2},{0,3},{1,4},{2,5},{3,6},{4,7},{5,8},{6,9},{7,... | collective-permute-start | bytes 786440 | tf_op jit(solution)/shard_map/ppermute | solution.py:185
  10.5 1.2 copy-start
  11.7 1.2 copy-start.1
  13.0 0.7 copy-start.2
  13.6 1.2 copy-start.3
  14.9 0.7 copy-start.4
  20.4 32.9 %collective-permute-start.3 = (bf16[512,256]{1,0:T(8,128)(2,1)S(1)}, bf16[512,256]{1,0:T(8,128)(2,1)S(1)}, u32[]{:S(2)}, u32[]{:S(2)}) collective-permute-start(bf16[512,256]{1,0:T(8,128)(2,1)S(1)} %pad_maximum_fusion.refs_7_.refs_6_), channel_id=1, source_target_pairs={{28,0},{29,1},{30,2},{31,3},{0,4},{1,5},{2,6},{3,7},{4,8},{5,9},{6... | collective-permute-start | bytes 786440 | tf_op jit(solution)/shard_map/ppermute | solution.py:185
  20.5 32.8 %collective-permute-start.2 = (bf16[512,256]{1,0:T(8,128)(2,1)S(1)}, bf16[512,256]{1,0:T(8,128)(2,1)S(1)}, u32[]{:S(2)}, u32[]{:S(2)}) collective-permute-start(bf16[512,256]{1,0:T(8,128)(2,1)S(1)} %pad_maximum_fusion.refs_7_.refs_6_), channel_id=1, source_target_pairs={{27,0},{28,1},{29,2},{30,3},{31,4},{0,5},{1,6},{2,7},{3,8},{4,9},{... | collective-permute-start | bytes 786440 | tf_op jit(solution)/shard_map/ppermute | solution.py:185
  53.3 18.2 %collective-permute-start.6 = (bf16[512,256]{1,0:T(8,128)(2,1)S(1)}, bf16[512,256]{1,0:T(8,128)(2,1)S(1)}, u32[]{:S(2)}, u32[]{:S(2)}) collective-permute-start(bf16[512,256]{1,0:T(8,128)(2,1)S(1)} %get-tuple-element.25), channel_id=1, source_target_pairs={{7,0},{8,1},{9,2},{10,3},{11,4},{12,5},{13,6},{14,7},{15,8},{16,9}... | collective-permute-start | bytes 786440 | tf_op jit(solution)/shard_map/ppermute | solution.py:185
  53.3 19.9 %collective-permute-start.7 = (bf16[512,256]{1,0:T(8,128)(2,1)S(1)}, bf16[512,256]{1,0:T(8,128)(2,1)S(1)}, u32[]{:S(2)}, u32[]{:S(2)}) collective-permute-start(bf16[512,256]{1,0:T(8,128)(2,1)S(1)} %get-tuple-element.26), channel_id=1, source_target_pairs={{6,0},{7,1},{8,2},{9,3},{10,4},{11,5},{12,6},{13,7},{14,8},{15,9},... | collective-permute-start | bytes 786440 | tf_op jit(solution)/shard_map/ppermute | solution.py:185
  54.1 36.5 %collective-permute-start.10 = (bf16[512,256]{1,0:T(8,128)(2,1)S(1)}, bf16[512,256]{1,0:T(8,128)(2,1)S(1)}, u32[]{:S(2)}, u32[]{:S(2)}) collective-permute-start(bf16[512,256]{1,0:T(8,128)(2,1)S(1)} %get-tuple-element.30), channel_id=1, source_target_pairs={{5,0},{6,1},{7,2},{8,3},{9,4},{10,5},{11,6},{12,7},{13,8},{14,9},{... | collective-permute-start | bytes 786440 | tf_op jit(solution)/shard_map/ppermute | solution.py:185
  61.3 29.3 %collective-permute-start.11 = (bf16[512,256]{1,0:T(8,128)(2,1)S(1)}, bf16[512,256]{1,0:T(8,128)(2,1)S(1)}, u32[]{:S(2)}, u32[]{:S(2)}) collective-permute-start(bf16[512,256]{1,0:T(8,128)(2,1)S(1)} %get-tuple-element.31), channel_id=1, source_target_pairs={{4,0},{5,1},{6,2},{7,3},{8,4},{9,5},{10,6},{11,7},{12,8},{13,9},{1... | collective-permute-start | bytes 786440 | tf_op jit(solution)/shard_map/ppermute | solution.py:185
  74.0 23.9 %collective-permute-start.12 = (bf16[512,256]{1,0:T(8,128)(2,1)S(1)}, bf16[512,256]{1,0:T(8,128)(2,1)S(1)}, u32[]{:S(2)}, u32[]{:S(2)}) collective-permute-start(bf16[512,256]{1,0:T(8,128)(2,1)S(1)} %get-tuple-element.34), channel_id=1, source_target_pairs={{3,0},{4,1},{5,2},{6,3},{7,4},{8,5},{9,6},{10,7},{11,8},{12,9},{13... | collective-permute-start | bytes 786440 | tf_op jit(solution)/shard_map/ppermute | solution.py:185
  86.6 13.5 %collective-permute-start.13 = (bf16[512,256]{1,0:T(8,128)(2,1)S(1)}, bf16[512,256]{1,0:T(8,128)(2,1)S(1)}, u32[]{:S(2)}, u32[]{:S(2)}) collective-permute-start(bf16[512,256]{1,0:T(8,128)(2,1)S(1)} %get-tuple-element.35), channel_id=1, source_target_pairs={{2,0},{3,1},{4,2},{5,3},{6,4},{7,5},{8,6},{9,7},{10,8},{11,9},{12,... | collective-permute-start | bytes 786440 | tf_op jit(solution)/shard_map/ppermute | solution.py:185
  94.3 12.8 %collective-permute-start.15 = (bf16[512,256]{1,0:T(8,128)(2,1)S(1)}, bf16[512,256]{1,0:T(8,128)(2,1)S(1)}, u32[]{:S(2)}, u32[]{:S(2)}) collective-permute-start(bf16[512,256]{1,0:T(8,128)(2,1)S(1)} %get-tuple-element.38), channel_id=1, source_target_pairs={{1,0},{2,1},{3,2},{4,3},{5,4},{6,5},{7,6},{8,7},{9,8},{10,9},{11,1... | collective-permute-start | bytes 786440 | tf_op jit(solution)/shard_map/ppermute | solution.py:185
  95.0 32.2 %collective-permute-start.9 = (bf16[512,512]{1,0:T(8,128)(2,1)S(1)}, bf16[512,512]{1,0:T(8,128)(2,1)S(1)}, u32[]{:S(2)}, u32[]{:S(2)}) collective-permute-start(bf16[512,512]{1,0:T(8,128)(2,1)S(1)} %get-tuple-element.28), channel_id=1, source_target_pairs={{32,0},{64,32},{96,64},{0,96},{33,1},{65,33},{97,65},{1,97},{34,2}... | collective-permute-start | bytes 1572872 | tf_op jit(solution)/shard_map/ppermute | solution.py:185
  104.4 22.8 %collective-permute-start.14 = (bf16[512,512]{1,0:T(8,128)(2,1)S(1)}, bf16[512,512]{1,0:T(8,128)(2,1)S(1)}, u32[]{:S(2)}, u32[]{:S(2)}) collective-permute-start(bf16[512,512]{1,0:T(8,128)(2,1)S(1)} %get-tuple-element.36), channel_id=1, source_target_pairs={{32,0},{64,32},{96,64},{0,96},{33,1},{65,33},{97,65},{1,97},{34,2}... | collective-permute-start | bytes 1572872 | tf_op jit(solution)/shard_map/ppermute | solution.py:185
  107.3 19.2 %collective-permute-start.16 = (bf16[512,256]{1,0:T(8,128)(2,1)S(1)}, bf16[512,256]{1,0:T(8,128)(2,1)S(1)}, u32[]{:S(2)}, u32[]{:S(2)}) collective-permute-start(bf16[512,256]{1,0:T(8,128)(2,1)S(1)} %add_convert_fusion), channel_id=1, source_target_pairs={{32,0},{64,32},{96,64},{0,96},{33,1},{65,33},{97,65},{1,97},{34,2}... | collective-permute-start | bytes 786440 | tf_op jit(solution)/shard_map/ppermute | solution.py:185
where the time goes:
time: 127 us; the launch traced here: 128 us
  waiting for transfers between devices  50.3 us (40%)
  starting transfers between devices  50.1 us (39%)
  Pallas kernels  19 us (15%)
  local copies, waits for them, and re-layouts  5.79 us (5%)
  other arithmetic  2.38 us (2%)
    ppermute x17, waiting for transfers between devices, shifted(): return lax.ppermute(block, axis, route)  50.3 us
    ppermute x17, starting transfers between devices, shifted(): return lax.ppermute(block, axis, route)  50.1 us
    pallas_call x7, Pallas kernels, call(): pl.pallas_call(kernel, out_shape=outs, in_specs=[pl.BlockSpec(memory_spac...  19 us
    unnamed x10, local copies, waits for them, and re-layouts  5.07 us
  transfers between devices with their start and end apart: 17, of which 5 were waited for; matrix products, arithmetic and copies ran while one was open for 1% of the time, Pallas kernels for 15%

commit v1 on v0

v1 whole, which is shorter than its diff:
```python
import math

import jax
import jax.numpy as jnp
from jax import lax
from jax.experimental import pallas as pl
from jax.experimental.pallas import tpu as pltpu
from jax.sharding import PartitionSpec as P

HEADS = 8
HD = 128
ROWS = 512
HALF = 256
SCALE = HD**-0.5
LOG2E = math.log2(math.e)
F32 = jnp.float32
BF16 = jnp.bfloat16
LSE, DELTA, LSE_BACK = 0, HEADS, 2 * HEADS
FAR = 4
SPLIT = 6
UNROLL = 4
WIDE = jax.ShapeDtypeStruct((HEADS * HD, ROWS), F32)
PAIR = jax.ShapeDtypeStruct((ROWS, 2 * HD), F32)


def dot(a, b, da, db):
    return lax.dot_general(a, b, (((da,), (db,)), ((), ())), preferred_element_type=F32)


def lanes(h):
    return pl.ds(pl.multiple_of(h * HD, HD), HD)


def terms(refs, h, to_h, lse_at, keys_at, n_keys, rows, ok):
    q_ref, do_ref, ld_ref, kv_ref, kt_ref, dq_ref, dk_ref, dv_ref = refs
    here = pl.ds(keys_at, n_keys)
    q = q_ref[rows, lanes(h)]
    do = do_ref[rows, lanes(h)]
    x = dot(kv_ref[here, :HD], q, 1, 1) * (SCALE * LOG2E) - ld_ref[pl.ds(lse_at + h, 1), rows]
    p = jnp.exp2(x)
    if ok is not None:
        p = jnp.where(ok, p, 0.0)
    dp = dot(kv_ref[here, HD:], do, 1, 1) - ld_ref[pl.ds(DELTA + h, 1), rows]
    ds = (p * dp).astype(BF16)
    dv_ref[here, :] += dot(p.astype(BF16), do, 1, 0)
    dk_ref[here, :] += dot(ds, q, 1, 0)
    dq_ref[lanes(to_h), rows] += dot(kt_ref[:, here], ds, 1, 0)


def finish(dq_ref, q_out):
    for h in range(q_out.shape[1] // HD):
        cols = slice(h * HD, (h + 1) * HD)
        q_out[:, cols] = (dq_ref[cols, :] * SCALE).astype(BF16).T


def own_terms(first, n, to, start_row, base, refs):
    kv_ref, kt_ref = refs[3], refs[4]
    kt_ref[...] = kv_ref[:, :HD].T

    def head(h, carry):
        for at, rows in ((0, slice(0, ROWS)), (HALF, slice(HALF, ROWS))):
            n_rows = rows.stop - rows.start
            key = lax.broadcasted_iota(jnp.int32, (HALF, n_rows), 0)
            ok = key >= start_row[:, rows] - (base + at)
            ok = ok & (key + (at - rows.start) <= lax.broadcasted_iota(jnp.int32, (HALF, n_rows), 1))
            terms(refs, h, h - to, LSE, at, HALF, rows, ok)
        return carry

    lax.fori_loop(first, first + n, head, 0)


def first_kernel(n, base_ref, starts, start_row, q_ref, do_ref, o_ref, lse_ref, kv_ref, ld_ref, dq_ref, out_ref, copy_ref, kt_ref, dk_ref, dv_ref):
    copy_ref[...] = kv_ref[...]
    lse = lse_ref[...] * LOG2E
    ld_ref[LSE : LSE + HEADS, :] = lse
    ld_ref[LSE_BACK : LSE_BACK + HEADS, :] = jnp.where(start_row[...] == starts[0, 0], lse, 1e30)
    ones = jnp.ones((8, HD), BF16)
    for h in range(HEADS):
        cols = slice(h * HD, (h + 1) * HD)
        x = do_ref[:, cols].astype(F32) * o_ref[:, cols].astype(F32)
        hi = x.astype(BF16)
        lo = (x - hi.astype(F32)).astype(BF16)
        row = dot(ones, hi, 1, 1) + dot(ones, lo, 1, 1)
        ld_ref[DELTA + h : DELTA + h + 1, :] = row[:1]
    dq_ref[...] = jnp.zeros_like(dq_ref)
    dk_ref[...] = jnp.zeros_like(dk_ref)
    dv_ref[...] = jnp.zeros_like(dv_ref)
    own_terms(0, n, 0, start_row, base_ref[0], (q_ref, do_ref, ld_ref, kv_ref, kt_ref, dq_ref, dk_ref, dv_ref))
    out_ref[:, :HD] = dk_ref[...]
    out_ref[:, HD:] = dv_ref[...]


def last_kernel(first, base_ref, starts, start_row, q_ref, do_ref, ld_ref, kv_ref, dq_in, sum_in, far_ref, part_ref, q_out, out_ref, passed_ref, dq_ref, kt_ref, dk_ref, dv_ref):
    dq_ref[...] = dq_in[first * HD :, :]
    dk_ref[...] = sum_in[:, :HD]
    dv_ref[...] = sum_in[:, HD:]
    own_terms(first, HEADS - first, first, start_row, base_ref[0], (q_ref, do_ref, ld_ref, kv_ref, kt_ref, dq_ref, dk_ref, dv_ref))
    finish(dq_ref, q_out)
    passed_ref[...] = far_ref[...].astype(F32) + part_ref[:ROWS, :].astype(F32)
    out_ref[:, :HD] = dk_ref[...] * SCALE + part_ref[ROWS:, :HD].astype(F32)
    out_ref[:, HD:] = dv_ref[...] + part_ref[ROWS:, HD:].astype(F32)


def back_kernel(ds, emit, joined, send, base_ref, starts, start_row, q_ref, do_ref, ld_ref, dq_in, *rest):
    m = len(ds)
    kv_in, rest = rest[:m], rest[m:]
    *rest, kv_ref, kt_ref, dk_ref, dv_ref = rest
    for i in range(send):
        rest[i - send][...] = rest[joined + i][...]
    rest = rest[: len(rest) - send]
    if emit:
        *rest, q_out = rest
    dq_ref, *out_refs = rest[-1 - m :] if emit else rest[-2:]
    base, start = base_ref[0], starts[0, 0]
    dk_ref[...] = jnp.zeros_like(dk_ref)
    dv_ref[...] = jnp.zeros_like(dv_ref)
    if joined:
        out_refs[0][m * ROWS :, :] = rest[0][...]
    reach = lax.shift_right_logical(base - start + (ROWS - 1), 9)
    skipped = sum((d > reach).astype(jnp.int32) for d in ds)
    refs = (q_ref, do_ref, ld_ref, kv_ref, kt_ref, dq_ref, dk_ref, dv_ref)

    def seen(d, width):
        key = lax.broadcasted_iota(jnp.int32, (ROWS, width), 0)
        return key >= start - (base - d * ROWS)

    @pl.when(skipped < m)
    def _():
        for b, d in enumerate(ds):
            here = slice(b * ROWS, (b + 1) * ROWS)
            kv = kv_in[b][...].astype(F32)
            kv_ref[here, :] = jnp.where(seen(d, 2 * HD), kv, kv[ROWS - 1 :, :]).astype(BF16)
            kt_ref[:, here] = jnp.where(seen(d, HD), kv[:, :HD], 0.0).astype(BF16).T

        def step(w, carry):
            w = w * UNROLL
            keys_at = pl.multiple_of((skipped + w // HEADS) * ROWS, ROWS)
            for i in range(UNROLL):
                h = w % HEADS + i
                terms(refs, h, h, LSE_BACK, keys_at, ROWS, slice(0, ROWS), None)
            return carry

        lax.fori_loop(0, (m - skipped) * (HEADS // UNROLL), step, 0)

    for b, d in enumerate(ds):
        here = slice(b * ROWS, (b + 1) * ROWS)
        ok = seen(d, HD)
        out_ref, to = (out_refs[b], slice(0, ROWS)) if emit else (out_refs[0], here)
        out_ref[to, :HD] = jnp.where(ok, dk_ref[here, :] * SCALE, 0.0).astype(BF16)
        out_ref[to, HD:] = jnp.where(ok, dv_ref[here, :], 0.0).astype(BF16)
    if emit:
        finish(dq_ref, q_out)


def work(pairs):
    flops = int(pairs * 5 * 2 * ROWS * ROWS * HD * HEADS * 0.05)
    return pl.CostEstimate(flops=flops, bytes_accessed=1 << 10, transcendentals=0)


def scratch(m):
    return [pltpu.VMEM((HD, m * ROWS), BF16), pltpu.VMEM((m * ROWS, HD), F32), pltpu.VMEM((m * ROWS, HD), F32)]


def call(kernel, name, pairs, scalars, operands, outs, scratch_shapes=(), aliases=None):
    return pl.pallas_call(
        kernel,
        out_shape=outs,
        in_specs=[pl.BlockSpec(memory_space=pltpu.SMEM)] * len(scalars) + [pl.BlockSpec(memory_space=pltpu.VMEM)] * len(operands),
        out_specs=[pl.BlockSpec(memory_space=pltpu.VMEM)] * len(outs),
        input_output_aliases=aliases or {},
        scratch_shapes=list(scratch_shapes),
        compiler_params=pltpu.CompilerParams(vmem_limit_bytes=24 << 20),
        cost_estimate=work(pairs),
        name=name,
    )(*scalars, *operands)


def shifted(block, axis, distance):
    devices = range(lax.axis_size(axis))
    route = [((i - distance) % len(devices), i) for i in devices]
    return lax.ppermute(block, axis, route)


def sum_kernel(total_ref, back_2, *rest):
    *arrays, out_ref = rest
    total = total_ref[...] + back_2[ROWS:, :].astype(F32)
    for array in arrays[:3]:
        total += array[...].astype(F32)
    out_ref[...] = total.astype(BF16)


def per_device(queries, keys, values, outputs, out_grads, lse, doc_start):
    q, do = queries[0], out_grads[0]
    base = (lax.axis_index("ctx") * ROWS).astype(jnp.int32)[None]
    kv = jnp.concatenate([keys[0], values[0]], axis=1)
    part = jax.ShapeDtypeStruct((ROWS, 2 * HD), BF16)
    pair = jax.ShapeDtypeStruct((2 * ROWS, 2 * HD), BF16)
    stats = jax.ShapeDtypeStruct((3 * HEADS, ROWS), F32)
    q_first = jax.ShapeDtypeStruct((ROWS, SPLIT * HD), BF16)
    q_last = jax.ShapeDtypeStruct((ROWS, (HEADS - SPLIT) * HD), BF16)
    scalars = (base, doc_start)

    def to_come(block, by):
        return shifted(block, "ctx", by)

    def first(*refs):
        first_kernel(SPLIT, *refs)

    held = {1: to_come(kv, 1), FAR: to_come(kv, FAR)}
    ld, dq, own, copy = call(
        first, "own_first", 0.6, scalars, (doc_start, q, do, outputs[0], lse[0].T, kv), [stats, WIDE, PAIR, part], scratch(1)
    )
    common = (doc_start, q, do, ld)

    def back(ds, dq, joined=(), emit=0, send=()):
        def kernel(*refs):
            back_kernel(ds, emit, len(joined), len(send), *refs)

        m = len(ds)
        outs = [part] * m if emit else [pair if m + len(joined) == 2 else part]
        return call(
            kernel,
            "back_" + "_".join(map(str, ds)),
            m,
            scalars,
            (*common, dq, *[held[d] for d in ds], *joined, *send),
            [WIDE] + outs + [q_first] * (emit > 0) + [part] * len(send),
            [pltpu.VMEM((m * ROWS, 2 * HD), BF16)] + scratch(m),
            {6: 0},
        )

    held[2] = to_come(copy, 2)
    dq, sum_1, copy, one = back((1,), dq, send=(kv, held[1]))
    held[3] = to_come(copy, 3)
    held[5] = to_come(one, FAR)
    dq, sum_4, two = back((4,), dq, send=(held[2],))
    held[6] = to_come(two, FAR)
    dq, sums, three = back((5,), dq, joined=(sum_1,), send=(held[3],))
    held[7] = to_come(three, FAR)
    back_1 = shifted(sums, "ctx", -1)
    dq, sums = back((6, 2), dq)
    back_2 = shifted(sums, "ctx", -2)
    dq, sum_7, sum_3, q_a = back((7, 3), dq, emit=SPLIT)
    back_7 = shifted(sum_7, "ctx", -7)
    back_3 = shifted(sum_3, "ctx", -3)
    handed_a = shifted(q_a, "section", -1)

    def final(*refs):
        last_kernel(SPLIT, *refs)

    q_b, total, passed = call(
        final,
        "own_last",
        0.4,
        scalars,
        (*common, kv, dq, own, sum_4, back_1),
        [q_last, PAIR, PAIR],
        [pltpu.VMEM(((HEADS - SPLIT) * HD, ROWS), F32)] + scratch(1),
    )
    handed_b = shifted(q_b, "section", -1)
    back_4 = shifted((passed + back_2[:ROWS].astype(F32)).astype(BF16), "ctx", -FAR)
    (kv_g,) = call(sum_kernel, "sums", 0.1, (), (total, back_2, back_7, back_3, back_4, handed_a), [part])
    kv_g = shifted(kv_g, "section", -1)
    return (jnp.concatenate([handed_a, handed_b], axis=1)[None], kv_g[None, :, :HD], kv_g[None, :, HD:])


def solution(mesh):
    wide = P("section", "ctx", None)
    in_specs = (wide, wide, wide, wide, wide, wide, P("section", "ctx"))
    return jax.shard_map(per_device, mesh=mesh, in_specs=in_specs, out_specs=(wide, wide, wide), check_vma=False)
```

time: 127 us -> 105 us (0.83); the launches traced: 128 us -> 105 us
  starting transfers between devices: 50.1 us -> 31.3 us
  waiting for transfers between devices: 50.3 us -> 35.1 us
  Pallas kernels: 19 us -> 29.6 us
    ppermute x17 -> x15, starting transfers between devices: 50.1 us -> 31.3 us  [shifted(): return lax.ppermute(block, axis, route)]
    ppermute x17 -> x15, waiting for transfers between devices: 50.3 us -> 35.1 us  [shifted(): return lax.ppermute(block, axis, route)]
    pallas_call x7 -> x8, Pallas kernels: 19 us -> 29.6 us  [call(): pl.pallas_call(kernel, out_shape=outs, in_specs=[pl.BlockSpec(memory_spac...]
  transfers between devices with their start and end apart: 17 -> 15, of which waited for: 5 -> 7; matrix products, arithmetic and copies ran while one was open for 1% -> 1% of each run, Pallas kernels for 15% -> 28%
where the time goes in v1:
time: 105 us
  waiting for transfers between devices  35.1 us (33%)
  starting transfers between devices  31.3 us (30%)
  Pallas kernels  29.6 us (28%)
  local copies, waits for them, and re-layouts  5.79 us (6%)
  other arithmetic  2.18 us (2%)
    ppermute x15, waiting for transfers between devices, shifted(): return lax.ppermute(block, axis, route)  35.1 us
    ppermute x15, starting transfers between devices, shifted(): return lax.ppermute(block, axis, route)  31.3 us
    pallas_call x8, Pallas kernels, call(): pl.pallas_call(kernel, out_shape=outs, in_specs=[pl.BlockSpec(memory_spac...  29.6 us
    unnamed x10, local copies, waits for them, and re-layouts  5.07 us
  transfers between devices with their start and end apart: 15, of which 7 were waited for; matrix products, arithmetic and copies ran while one was open for 1% of the time, Pallas kernels for 28%

profile of v1, /device:TPU:31, one launch (start us, length us, event | category | flops | bytes accessed | tf_op | source)
XLA Modules:
  0.0 104.7 jit_solution(16155775087226573158)
XLA Ops:
  1.6 1.3 %collective-permute-start = (bf16[512,256]{1,0:T(8,128)(2,1)S(1)}, bf16[512,256]{1,0:T(8,128)(2,1)S(1)}, u32[]{:S(2)}, u32[]{:S(2)}) collective-permute-start(bf16[512,256]{1,0:T(8,128)(2,1)S(1)} %pad_maximum_fusion.refs_7_.refs_8_.refs_6_), channel_id=1, source_target_pairs={{31,0},{0,1},{1,2},{2,3},{3,4},{4,5},{5,6},{6,7},{7,8},{8,9},{9,10... | collective-permute-start | bytes 786440 | tf_op jit(solution)/shard_map/ppermute | solution.py:181
  2.9 1.2 %collective-permute-start.1 = (bf16[512,256]{1,0:T(8,128)(2,1)S(1)}, bf16[512,256]{1,0:T(8,128)(2,1)S(1)}, u32[]{:S(2)}, u32[]{:S(2)}) collective-permute-start(bf16[512,256]{1,0:T(8,128)(2,1)S(1)} %pad_maximum_fusion.refs_7_.refs_8_.refs_6_), channel_id=1, source_target_pairs={{28,0},{29,1},{30,2},{31,3},{0,4},{1,5},{2,6},{3,7},{4,8},{5,9},{6... | collective-permute-start | bytes 786440 | tf_op jit(solution)/shard_map/ppermute | solution.py:181
  4.1 1.2 %copy-done = bf16[1,512,1024]{2,1,0:T(8,128)(2,1)S(1)} copy-done((bf16[1,512,1024]{2,1,0:T(8,128)(2,1)S(1)}, bf16[1,512,1024]{2,1,0:T(8,128)(2,1)}, u32[]{:S(2)}) %copy-start) | copy-done | bytes 1048600
  5.3 1.2 %copy-done.1 = bf16[1,512,1024]{2,1,0:T(8,128)(2,1)S(1)} copy-done((bf16[1,512,1024]{2,1,0:T(8,128)(2,1)S(1)}, bf16[1,512,1024]{2,1,0:T(8,128)(2,1)}, u32[]{:S(2)}) %copy-start.1) | copy-done | bytes 1048600
  6.6 1.2 %copy-done.2 = bf16[1,512,1024]{2,1,0:T(8,128)(2,1)S(1)} copy-done((bf16[1,512,1024]{2,1,0:T(8,128)(2,1)S(1)}, bf16[1,512,1024]{2,1,0:T(8,128)(2,1)}, u32[]{:S(2)}) %copy-start.2) | copy-done | bytes 1048600
  9.2 6.5 %own_first.1 = (f32[24,512]{1,0:T(8,128)S(1)}, f32[1024,512]{1,0:T(8,128)S(1)}, f32[512,256]{1,0:T(8,128)S(1)}, bf16[512,256]{1,0:T(8,128)(2,1)S(1)}) custom-call(s32[1]{0:T(128)} %bitcast.refs_0_, s32[1,512]{1,0:T(1,128)S(1)} %copy-done.3, s32[1,512]{1,0:T(1,128)S(1)} %copy-done.3, bf16[512,1024]{1,0:T(8,128)(2,1)S(1)} %bitcast.15, ...), custom_call_target="tpu_custom_call" | custom-call | flops 80530640 | bytes 1024 | tf_op jit(solution)/shard_map/own_first/pallas_call | solution.py:165
  15.7 2.4 %collective-permute-start.2 = (bf16[512,256]{1,0:T(8,128)(2,1)S(1)}, bf16[512,256]{1,0:T(8,128)(2,1)S(1)}, u32[]{:S(2)}, u32[]{:S(2)}) collective-permute-start(bf16[512,256]{1,0:T(8,128)(2,1)S(1)} %get-tuple-element.29), channel_id=1, source_target_pairs={{30,0},{31,1},{0,2},{1,3},{2,4},{3,5},{4,6},{5,7},{6,8},{7,9},{8,1... | collective-permute-start | bytes 786440 | tf_op jit(solution)/shard_map/ppermute | solution.py:181
  18.0 6.1 %back_1.1 = (f32[1024,512]{1,0:T(8,128)S(1)}, bf16[512,256]{1,0:T(8,128)(2,1)S(1)}, bf16[512,256]{1,0:T(8,128)(2,1)S(1)}, bf16[512,256]{1,0:T(8,128)(2,1)S(1)}) custom-call(s32[1]{0:T(128)} %bitcast.refs_0_, s32[1,512]{1,0:T(1,128)S(1)} %copy-done.3, s32[1,512]{1,0:T(1,128)S(1)} %copy-done.3, ...), custom_call_target="tpu_custom_call", output_to_operand_aliasing={{0}: (6, {})} | custom-call | flops 134217728 | bytes 1024 | tf_op jit(solution)/shard_map/back_1/pallas_call | solution.py:165
  24.2 1.3 %collective-permute-start.3 = (bf16[512,256]{1,0:T(8,128)(2,1)S(1)}, bf16[512,256]{1,0:T(8,128)(2,1)S(1)}, u32[]{:S(2)}, u32[]{:S(2)}) collective-permute-start(bf16[512,256]{1,0:T(8,128)(2,1)S(1)} %get-tuple-element.31), channel_id=1, source_target_pairs={{28,0},{29,1},{30,2},{31,3},{0,4},{1,5},{2,6},{3,7},{4,8},{5,9},{6... | collective-permute-start | bytes 786440 | tf_op jit(solution)/shard_map/ppermute | solution.py:181
  27.2 3.4 %collective-permute-done.3.refs_7_ = bf16[512,256]{1,0:T(8,128)(2,1)S(1)} collective-permute-done((bf16[512,256]{1,0:T(8,128)(2,1)S(1)}, bf16[512,256]{1,0:T(8,128)(2,1)S(1)}, u32[]{:S(2)}, u32[]{:S(2)}) %collective-permute-start.3) | collective-permute-done | bytes 262176 | tf_op jit(solution)/shard_map/ppermute | solution.py:181
  30.5 4.6 %collective-permute-done.4.refs_9_.refs_8_ = bf16[512,256]{1,0:T(8,128)(2,1)S(1)} collective-permute-done((bf16[512,256]{1,0:T(8,128)(2,1)S(1)}, bf16[512,256]{1,0:T(8,128)(2,1)S(1)}, u32[]{:S(2)}, u32[]{:S(2)}) %collective-permute-start.4) | collective-permute-done | bytes 262176 | tf_op jit(solution)/shard_map/ppermute | solution.py:181
  37.0 5.1 %collective-permute-start.8 = (bf16[1024,256]{1,0:T(8,128)(2,1)S(1)}, bf16[1024,256]{1,0:T(8,128)(2,1)S(1)}, u32[]{:S(2)}, u32[]{:S(2)}) collective-permute-start(bf16[1024,256]{1,0:T(8,128)(2,1)S(1)} %get-tuple-element.42), channel_id=1, source_target_pairs={{1,0},{2,1},{3,2},{4,3},{5,4},{6,5},{7,6},{8,7},{9,8},{10,9},{11,1... | collective-permute-start | bytes 1572872 | tf_op jit(solution)/shard_map/ppermute | solution.py:181
  42.2 6.3 %back_6_2.1 = (f32[1024,512]{1,0:T(8,128)S(1)}, bf16[1024,256]{1,0:T(8,128)(2,1)S(1)}) custom-call(s32[1]{0:T(128)} %bitcast.refs_0_, s32[1,512]{1,0:T(1,128)S(1)} %copy-done.3, s32[1,512]{1,0:T(1,128)S(1)} %copy-done.3, bf16[512,1024]{1,0:T(8,128)(2,1)S(1)} %bitcast.19, bf16[512,1024]{1,0:T(8,128)(2,1)S(1)} %bitcast.26, ...), custom_call_target="tpu_custom_call", output_to_operand_aliasing={{0}: (6, {})} | custom-call | flops 268435456 | bytes 1024 | tf_op jit(solution)/shard_map/back_6_2/pallas_call | solution.py:165
  48.6 6.6 %back_7_3.1 = (f32[1024,512]{1,0:T(8,128)S(1)}, bf16[512,256]{1,0:T(8,128)(2,1)S(1)}, bf16[512,256]{1,0:T(8,128)(2,1)S(1)}, bf16[512,768]{1,0:T(8,128)(2,1)S(1)}) custom-call(s32[1]{0:T(128)} %bitcast.refs_0_, s32[1,512]{1,0:T(1,128)S(1)} %copy-done.3, s32[1,512]{1,0:T(1,128)S(1)} %copy-done.3, ...), custom_call_target="tpu_custom_call", output_to_operand_aliasing={{0}: (6, {})} | custom-call | flops 268435456 | bytes 1024 | tf_op jit(solution)/shard_map/back_7_3/pallas_call | solution.py:165
  55.1 3.2 %collective-permute-start.7 = (bf16[512,768]{1,0:T(8,128)(2,1)S(1)}, bf16[512,768]{1,0:T(8,128)(2,1)S(1)}, u32[]{:S(2)}, u32[]{:S(2)}) collective-permute-start(bf16[512,768]{1,0:T(8,128)(2,1)S(1)} %get-tuple-element.38), channel_id=1, source_target_pairs={{32,0},{64,32},{96,64},{0,96},{33,1},{65,33},{97,65},{1,97},{34,2}... | collective-permute-start | bytes 2359304 | tf_op jit(solution)/shard_map/ppermute | solution.py:181
  58.3 4.6 %collective-permute-start.11 = (bf16[512,256]{1,0:T(8,128)(2,1)S(1)}, bf16[512,256]{1,0:T(8,128)(2,1)S(1)}, u32[]{:S(2)}, u32[]{:S(2)}) collective-permute-start(bf16[512,256]{1,0:T(8,128)(2,1)S(1)} %get-tuple-element.46), channel_id=1, source_target_pairs={{7,0},{8,1},{9,2},{10,3},{11,4},{12,5},{13,6},{14,7},{15,8},{16,9}... | collective-permute-start | bytes 786440 | tf_op jit(solution)/shard_map/ppermute | solution.py:181
  62.9 2.6 %collective-permute-start.12 = (bf16[512,256]{1,0:T(8,128)(2,1)S(1)}, bf16[512,256]{1,0:T(8,128)(2,1)S(1)}, u32[]{:S(2)}, u32[]{:S(2)}) collective-permute-start(bf16[512,256]{1,0:T(8,128)(2,1)S(1)} %get-tuple-element.47), channel_id=1, source_target_pairs={{3,0},{4,1},{5,2},{6,3},{7,4},{8,5},{9,6},{10,7},{11,8},{12,9},{13... | collective-permute-start | bytes 786440 | tf_op jit(solution)/shard_map/ppermute | solution.py:181
  65.5 2.6 %own_last.1 = (bf16[512,256]{1,0:T(8,128)(2,1)S(1)}, f32[512,256]{1,0:T(8,128)S(1)}, f32[512,256]{1,0:T(8,128)S(1)}) custom-call(s32[1]{0:T(128)} %bitcast.refs_0_, s32[1,512]{1,0:T(1,128)S(1)} %copy-done.3, s32[1,512]{1,0:T(1,128)S(1)} %copy-done.3, bf16[512,1024]{1,0:T(8,128)(2,1)S(1)} %bitcast.21, bf16[512,1024]{1,0:T(8,128)(2,1)S(1)} %bitcast.28, ...), custom_call_target="tpu_custom_call" | custom-call | flops 53687092 | bytes 1024 | tf_op jit(solution)/shard_map/own_last/pallas_call | solution.py:165
  68.1 1.8 %collective-permute-done.10.back_2 = bf16[1024,256]{1,0:T(8,128)(2,1)S(1)} collective-permute-done((bf16[1024,256]{1,0:T(8,128)(2,1)S(1)}, bf16[1024,256]{1,0:T(8,128)(2,1)S(1)}, u32[]{:S(2)}, u32[]{:S(2)}) %collective-permute-start.10) | collective-permute-done | bytes 524320 | tf_op jit(solution)/shard_map/ppermute | solution.py:181
  70.0 7.3 %collective-permute-start.9 = (bf16[512,256]{1,0:T(8,128)(2,1)S(1)}, bf16[512,256]{1,0:T(8,128)(2,1)S(1)}, u32[]{:S(2)}, u32[]{:S(2)}) collective-permute-start(bf16[512,256]{1,0:T(8,128)(2,1)S(1)} %get-tuple-element.43), channel_id=1, source_target_pairs={{32,0},{64,32},{96,64},{0,96},{33,1},{65,33},{97,65},{1,97},{34,2}... | collective-permute-start | bytes 786440 | tf_op jit(solution)/shard_map/ppermute | solution.py:181
  77.3 10.8 %collective-permute-done.12.rest_1_ = bf16[512,256]{1,0:T(8,128)(2,1)S(1)} collective-permute-done((bf16[512,256]{1,0:T(8,128)(2,1)S(1)}, bf16[512,256]{1,0:T(8,128)(2,1)S(1)}, u32[]{:S(2)}, u32[]{:S(2)}) %collective-permute-start.12) | collective-permute-done | bytes 262176 | tf_op jit(solution)/shard_map/ppermute | solution.py:181
  88.1 8.3 %collective-permute-done.7.rest_3_ = bf16[512,768]{1,0:T(8,128)(2,1)S(1)} collective-permute-done((bf16[512,768]{1,0:T(8,128)(2,1)S(1)}, bf16[512,768]{1,0:T(8,128)(2,1)S(1)}, u32[]{:S(2)}, u32[]{:S(2)}) %collective-permute-start.7) | collective-permute-done | bytes 786464 | tf_op jit(solution)/shard_map/ppermute | solution.py:181
  96.7 2.6 %collective-permute-done.9 = bf16[512,256]{1,0:T(8,128)(2,1)S(1)} collective-permute-done((bf16[512,256]{1,0:T(8,128)(2,1)S(1)}, bf16[512,256]{1,0:T(8,128)(2,1)S(1)}, u32[]{:S(2)}, u32[]{:S(2)}) %collective-permute-start.9) | collective-permute-done | bytes 262176 | tf_op jit(solution)/shard_map/ppermute | solution.py:181
  100.3 3.6 %collective-permute-done.14 = bf16[512,256]{1,0:T(8,128)(2,1)S(1)} collective-permute-done((bf16[512,256]{1,0:T(8,128)(2,1)S(1)}, bf16[512,256]{1,0:T(8,128)(2,1)S(1)}, u32[]{:S(2)}, u32[]{:S(2)}) %collective-permute-start.14) | collective-permute-done | bytes 262176 | tf_op jit(solution)/shard_map/ppermute | solution.py:181
  (28 shorter events, 8.2 us)
Async XLA Ops:
  1.6 16.4 %collective-permute-start = (bf16[512,256]{1,0:T(8,128)(2,1)S(1)}, bf16[512,256]{1,0:T(8,128)(2,1)S(1)}, u32[]{:S(2)}, u32[]{:S(2)}) collective-permute-start(bf16[512,256]{1,0:T(8,128)(2,1)S(1)} %pad_maximum_fusion.refs_7_.refs_8_.refs_6_), channel_id=1, source_target_pairs={{31,0},{0,1},{1,2},{2,3},{3,4},{4,5},{5,6},{6,7},{7,8},{8,9},{9,10... | collective-permute-start | bytes 786440 | tf_op jit(solution)/shard_map/ppermute | solution.py:181
  2.9 22.7 %collective-permute-start.1 = (bf16[512,256]{1,0:T(8,128)(2,1)S(1)}, bf16[512,256]{1,0:T(8,128)(2,1)S(1)}, u32[]{:S(2)}, u32[]{:S(2)}) collective-permute-start(bf16[512,256]{1,0:T(8,128)(2,1)S(1)} %pad_maximum_fusion.refs_7_.refs_8_.refs_6_), channel_id=1, source_target_pairs={{28,0},{29,1},{30,2},{31,3},{0,4},{1,5},{2,6},{3,7},{4,8},{5,9},{6... | collective-permute-start | bytes 786440 | tf_op jit(solution)/shard_map/ppermute | solution.py:181
  4.1 1.2 %copy-start = (bf16[1,512,1024]{2,1,0:T(8,128)(2,1)S(1)}, bf16[1,512,1024]{2,1,0:T(8,128)(2,1)}, u32[]{:S(2)}) copy-start(bf16[1,512,1024]{2,1,0:T(8,128)(2,1)} %param.7) | copy-start | bytes 3145732
  5.3 1.2 %copy-start.1 = (bf16[1,512,1024]{2,1,0:T(8,128)(2,1)S(1)}, bf16[1,512,1024]{2,1,0:T(8,128)(2,1)}, u32[]{:S(2)}) copy-start(bf16[1,512,1024]{2,1,0:T(8,128)(2,1)} %param.11) | copy-start | bytes 3145732
  6.6 1.2 %copy-start.2 = (bf16[1,512,1024]{2,1,0:T(8,128)(2,1)S(1)}, bf16[1,512,1024]{2,1,0:T(8,128)(2,1)}, u32[]{:S(2)}) copy-start(bf16[1,512,1024]{2,1,0:T(8,128)(2,1)} %param.10) | copy-start | bytes 3145732
  7.8 0.7 copy-start.3
  8.5 0.7 copy-start.4
  15.7 10.0 %collective-permute-start.2 = (bf16[512,256]{1,0:T(8,128)(2,1)S(1)}, bf16[512,256]{1,0:T(8,128)(2,1)S(1)}, u32[]{:S(2)}, u32[]{:S(2)}) collective-permute-start(bf16[512,256]{1,0:T(8,128)(2,1)S(1)} %get-tuple-element.29), channel_id=1, source_target_pairs={{30,0},{31,1},{0,2},{1,3},{2,4},{3,5},{4,6},{5,7},{6,8},{7,9},{8,1... | collective-permute-start | bytes 786440 | tf_op jit(solution)/shard_map/ppermute | solution.py:181
  24.2 6.4 %collective-permute-start.3 = (bf16[512,256]{1,0:T(8,128)(2,1)S(1)}, bf16[512,256]{1,0:T(8,128)(2,1)S(1)}, u32[]{:S(2)}, u32[]{:S(2)}) collective-permute-start(bf16[512,256]{1,0:T(8,128)(2,1)S(1)} %get-tuple-element.31), channel_id=1, source_target_pairs={{28,0},{29,1},{30,2},{31,3},{0,4},{1,5},{2,6},{3,7},{4,8},{5,9},{6... | collective-permute-start | bytes 786440 | tf_op jit(solution)/shard_map/ppermute | solution.py:181
  25.5 9.7 %collective-permute-start.4 = (bf16[512,256]{1,0:T(8,128)(2,1)S(1)}, bf16[512,256]{1,0:T(8,128)(2,1)S(1)}, u32[]{:S(2)}, u32[]{:S(2)}) collective-permute-start(bf16[512,256]{1,0:T(8,128)(2,1)S(1)} %get-tuple-element.33), channel_id=1, source_target_pairs={{29,0},{30,1},{31,2},{0,3},{1,4},{2,5},{3,6},{4,7},{5,8},{6,9},{7,... | collective-permute-start | bytes 786440 | tf_op jit(solution)/shard_map/ppermute | solution.py:181
  26.4 15.8 %collective-permute-start.5 = (bf16[512,256]{1,0:T(8,128)(2,1)S(1)}, bf16[512,256]{1,0:T(8,128)(2,1)S(1)}, u32[]{:S(2)}, u32[]{:S(2)}) collective-permute-start(bf16[512,256]{1,0:T(8,128)(2,1)S(1)} %get-tuple-element.35), channel_id=1, source_target_pairs={{28,0},{29,1},{30,2},{31,3},{0,4},{1,5},{2,6},{3,7},{4,8},{5,9},{6... | collective-permute-start | bytes 786440 | tf_op jit(solution)/shard_map/ppermute | solution.py:181
  35.9 12.7 %collective-permute-start.6 = (bf16[512,256]{1,0:T(8,128)(2,1)S(1)}, bf16[512,256]{1,0:T(8,128)(2,1)S(1)}, u32[]{:S(2)}, u32[]{:S(2)}) collective-permute-start(bf16[512,256]{1,0:T(8,128)(2,1)S(1)} %get-tuple-element.37), channel_id=1, source_target_pairs={{28,0},{29,1},{30,2},{31,3},{0,4},{1,5},{2,6},{3,7},{4,8},{5,9},{6... | collective-permute-start | bytes 786440 | tf_op jit(solution)/shard_map/ppermute | solution.py:181
  37.0 28.5 %collective-permute-start.8 = (bf16[1024,256]{1,0:T(8,128)(2,1)S(1)}, bf16[1024,256]{1,0:T(8,128)(2,1)S(1)}, u32[]{:S(2)}, u32[]{:S(2)}) collective-permute-start(bf16[1024,256]{1,0:T(8,128)(2,1)S(1)} %get-tuple-element.42), channel_id=1, source_target_pairs={{1,0},{2,1},{3,2},{4,3},{5,4},{6,5},{7,6},{8,7},{9,8},{10,9},{11,1... | collective-permute-start | bytes 1572872 | tf_op jit(solution)/shard_map/ppermute | solution.py:181
  48.5 21.4 %collective-permute-start.10 = (bf16[1024,256]{1,0:T(8,128)(2,1)S(1)}, bf16[1024,256]{1,0:T(8,128)(2,1)S(1)}, u32[]{:S(2)}, u32[]{:S(2)}) collective-permute-start(bf16[1024,256]{1,0:T(8,128)(2,1)S(1)} %get-tuple-element.45), channel_id=1, source_target_pairs={{2,0},{3,1},{4,2},{5,3},{6,4},{7,5},{8,6},{9,7},{10,8},{11,9},{12,... | collective-permute-start | bytes 1572872 | tf_op jit(solution)/shard_map/ppermute | solution.py:181
  55.1 41.3 %collective-permute-start.7 = (bf16[512,768]{1,0:T(8,128)(2,1)S(1)}, bf16[512,768]{1,0:T(8,128)(2,1)S(1)}, u32[]{:S(2)}, u32[]{:S(2)}) collective-permute-start(bf16[512,768]{1,0:T(8,128)(2,1)S(1)} %get-tuple-element.38), channel_id=1, source_target_pairs={{32,0},{64,32},{96,64},{0,96},{33,1},{65,33},{97,65},{1,97},{34,2}... | collective-permute-start | bytes 2359304 | tf_op jit(solution)/shard_map/ppermute | solution.py:181
  58.3 19.0 %collective-permute-start.11 = (bf16[512,256]{1,0:T(8,128)(2,1)S(1)}, bf16[512,256]{1,0:T(8,128)(2,1)S(1)}, u32[]{:S(2)}, u32[]{:S(2)}) collective-permute-start(bf16[512,256]{1,0:T(8,128)(2,1)S(1)} %get-tuple-element.46), channel_id=1, source_target_pairs={{7,0},{8,1},{9,2},{10,3},{11,4},{12,5},{13,6},{14,7},{15,8},{16,9}... | collective-permute-start | bytes 786440 | tf_op jit(solution)/shard_map/ppermute | solution.py:181
  62.9 25.2 %collective-permute-start.12 = (bf16[512,256]{1,0:T(8,128)(2,1)S(1)}, bf16[512,256]{1,0:T(8,128)(2,1)S(1)}, u32[]{:S(2)}, u32[]{:S(2)}) collective-permute-start(bf16[512,256]{1,0:T(8,128)(2,1)S(1)} %get-tuple-element.47), channel_id=1, source_target_pairs={{3,0},{4,1},{5,2},{6,3},{7,4},{8,5},{9,6},{10,7},{11,8},{12,9},{13... | collective-permute-start | bytes 786440 | tf_op jit(solution)/shard_map/ppermute | solution.py:181
  69.9 18.2 %collective-permute-start.13 = (bf16[512,256]{1,0:T(8,128)(2,1)S(1)}, bf16[512,256]{1,0:T(8,128)(2,1)S(1)}, u32[]{:S(2)}, u32[]{:S(2)}) collective-permute-start(bf16[512,256]{1,0:T(8,128)(2,1)S(1)} %add_convert_fusion), channel_id=1, source_target_pairs={{4,0},{5,1},{6,2},{7,3},{8,4},{9,5},{10,6},{11,7},{12,8},{13,9},{1... | collective-permute-start | bytes 786440 | tf_op jit(solution)/shard_map/ppermute | solution.py:181
  70.0 29.2 %collective-permute-start.9 = (bf16[512,256]{1,0:T(8,128)(2,1)S(1)}, bf16[512,256]{1,0:T(8,128)(2,1)S(1)}, u32[]{:S(2)}, u32[]{:S(2)}) collective-permute-start(bf16[512,256]{1,0:T(8,128)(2,1)S(1)} %get-tuple-element.43), channel_id=1, source_target_pairs={{32,0},{64,32},{96,64},{0,96},{33,1},{65,33},{97,65},{1,97},{34,2}... | collective-permute-start | bytes 786440 | tf_op jit(solution)/shard_map/ppermute | solution.py:181
  96.6 7.4 %collective-permute-start.14 = (bf16[512,256]{1,0:T(8,128)(2,1)S(1)}, bf16[512,256]{1,0:T(8,128)(2,1)S(1)}, u32[]{:S(2)}, u32[]{:S(2)}) collective-permute-start(bf16[512,256]{1,0:T(8,128)(2,1)S(1)} %sums.1), channel_id=1, source_target_pairs={{32,0},{64,32},{96,64},{0,96},{33,1},{65,33},{97,65},{1,97},{34,2}... | collective-permute-start | bytes 786440 | tf_op jit(solution)/shard_map/ppermute | solution.py:181

commit v2 on v1

--- a/solution.py
+++ b/solution.py
@@ -69,7 +69,7 @@
     lax.fori_loop(first, first + n, head, 0)
 
 
-def first_kernel(n, base_ref, starts, start_row, q_ref, do_ref, o_ref, lse_ref, kv_ref, ld_ref, dq_ref, out_ref, copy_ref, kt_ref, dk_ref, dv_ref):
+def first_kernel(starts, start_row, do_ref, o_ref, lse_ref, kv_ref, ld_ref, dq_ref, copy_ref):
     copy_ref[...] = kv_ref[...]
     lse = lse_ref[...] * LOG2E
     ld_ref[LSE : LSE + HEADS, :] = lse
@@ -83,6 +83,9 @@
         row = dot(ones, hi, 1, 1) + dot(ones, lo, 1, 1)
         ld_ref[DELTA + h : DELTA + h + 1, :] = row[:1]
     dq_ref[...] = jnp.zeros_like(dq_ref)
+
+
+def own_kernel(n, base_ref, starts, start_row, q_ref, do_ref, ld_ref, kv_ref, dq_in, dq_ref, out_ref, kt_ref, dk_ref, dv_ref):
     dk_ref[...] = jnp.zeros_like(dk_ref)
     dv_ref[...] = jnp.zeros_like(dv_ref)
     own_terms(0, n, 0, start_row, base_ref[0], (q_ref, do_ref, ld_ref, kv_ref, kt_ref, dq_ref, dk_ref, dv_ref))
@@ -203,13 +206,11 @@
     def to_come(block, by):
         return shifted(block, "ctx", by)
 
-    def first(*refs):
-        first_kernel(SPLIT, *refs)
+    def own_most(*refs):
+        own_kernel(SPLIT, *refs)
 
     held = {1: to_come(kv, 1), FAR: to_come(kv, FAR)}
-    ld, dq, own, copy = call(
-        first, "own_first", 0.6, scalars, (doc_start, q, do, outputs[0], lse[0].T, kv), [stats, WIDE, PAIR, part], scratch(1)
-    )
+    ld, dq, copy = call(first_kernel, "statistics", 0.1, (doc_start,), (doc_start, do, outputs[0], lse[0].T, kv), [stats, WIDE, part])
     common = (doc_start, q, do, ld)
 
     def back(ds, dq, joined=(), emit=0, send=()):
@@ -235,6 +236,7 @@
     held[5] = to_come(one, FAR)
     dq, sum_4, two = back((4,), dq, send=(held[2],))
     held[6] = to_come(two, FAR)
+    dq, own = call(own_most, "own_most", 0.6, scalars, (*common, kv, dq), [WIDE, PAIR], scratch(1), {7: 0})
     dq, sums, three = back((5,), dq, joined=(sum_1,), send=(held[3],))
     held[7] = to_come(three, FAR)
     back_1 = shifted(sums, "ctx", -1)

time: 105 us -> 105 us (level)
  the two profiles are of different devices: /device:TPU:31 before, /device:TPU:63 now
where the time goes in v2:
time: 105 us; the launch traced here: 104 us
  Pallas kernels  37.5 us (36%)
  waiting for transfers between devices  35.5 us (34%)
  starting transfers between devices  22.3 us (21%)
  local copies, waits for them, and re-layouts  5.79 us (6%)
  other arithmetic  2.18 us (2%)
    pallas_call x9, Pallas kernels, call(): pl.pallas_call(kernel, out_shape=outs, in_specs=[pl.BlockSpec(memory_spac...  37.5 us
    ppermute x15, waiting for transfers between devices, shifted(): return lax.ppermute(block, axis, route)  35.5 us
    ppermute x15, starting transfers between devices, shifted(): return lax.ppermute(block, axis, route)  22.3 us
    unnamed x14, local copies, waits for them, and re-layouts  5.08 us
  transfers between devices with their start and end apart: 15, of which 6 were waited for; matrix products, arithmetic and copies ran while one was open for 1% of the time, Pallas kernels for 36%

profile of v2, /device:TPU:63, one launch (start us, length us, event | category | flops | bytes accessed | tf_op | source)
XLA Modules:
  0.0 104.1 jit_solution(1615592282979310723)
XLA Ops:
  2.3 1.2 %copy-done = bf16[1,512,1024]{2,1,0:T(8,128)(2,1)S(1)} copy-done((bf16[1,512,1024]{2,1,0:T(8,128)(2,1)S(1)}, bf16[1,512,1024]{2,1,0:T(8,128)(2,1)}, u32[]{:S(2)}) %copy-start) | copy-done | bytes 1048600
  3.6 1.2 %copy-done.3 = bf16[1,512,1024]{2,1,0:T(8,128)(2,1)S(1)} copy-done((bf16[1,512,1024]{2,1,0:T(8,128)(2,1)S(1)}, bf16[1,512,1024]{2,1,0:T(8,128)(2,1)}, u32[]{:S(2)}) %copy-start.3) | copy-done | bytes 1048600
  6.2 2.0 %statistics.1 = (f32[24,512]{1,0:T(8,128)S(1)}, f32[1024,512]{1,0:T(8,128)S(1)}, bf16[512,256]{1,0:T(8,128)(2,1)}) custom-call(s32[1,512]{1,0:T(1,128)S(1)} %copy-done.4, s32[1,512]{1,0:T(1,128)S(1)} %copy-done.4, bf16[512,1024]{1,0:T(8,128)(2,1)S(1)} %bitcast.15, bf16[512,1024]{1,0:T(8,128)(2,1)S(1)} %bitcast.30, f32[8,512]{1,0:T(8,128)S(1)} %bitcast.31, ...), custom_call_target="tpu_custom_call" | custom-call | flops 13421772 | bytes 1024 | tf_op jit(solution)/shard_map/statistics/pallas_call | solution.py:168
  8.2 2.3 %collective-permute-start.2 = (bf16[512,256]{1,0:T(8,128)(2,1)}, bf16[512,256]{1,0:T(8,128)(2,1)}, u32[]{:S(2)}, u32[]{:S(2)}) collective-permute-start(bf16[512,256]{1,0:T(8,128)(2,1)} %get-tuple-element.30), channel_id=1, source_target_pairs={{30,0},{31,1},{0,2},{1,3},{2,4},{3,5},{4,6},{5,7},{6,8},{7,9},{8,1... | collective-permute-start | bytes 786440 | tf_op jit(solution)/shard_map/ppermute | solution.py:184
  10.5 1.2 %copy-done.2 = bf16[1,512,1024]{2,1,0:T(8,128)(2,1)S(1)} copy-done((bf16[1,512,1024]{2,1,0:T(8,128)(2,1)S(1)}, bf16[1,512,1024]{2,1,0:T(8,128)(2,1)}, u32[]{:S(2)}) %copy-start.2) | copy-done | bytes 1048600
  11.7 6.6 %back_1.1 = (f32[1024,512]{1,0:T(8,128)S(1)}, bf16[512,256]{1,0:T(8,128)(2,1)S(1)}, bf16[512,256]{1,0:T(8,128)(2,1)S(1)}, bf16[512,256]{1,0:T(8,128)(2,1)S(1)}) custom-call(s32[1]{0:T(128)} %bitcast.refs_0_, s32[1,512]{1,0:T(1,128)S(1)} %copy-done.5, s32[1,512]{1,0:T(1,128)S(1)} %copy-done.5, ...), custom_call_target="tpu_custom_call", output_to_operand_aliasing={{0}: (6, {})} | custom-call | flops 134217728 | bytes 1024 | tf_op jit(solution)/shard_map/back_1/pallas_call | solution.py:168
  18.3 1.3 %collective-permute-start.3 = (bf16[512,256]{1,0:T(8,128)(2,1)S(1)}, bf16[512,256]{1,0:T(8,128)(2,1)S(1)}, u32[]{:S(2)}, u32[]{:S(2)}) collective-permute-start(bf16[512,256]{1,0:T(8,128)(2,1)S(1)} %get-tuple-element.33), channel_id=1, source_target_pairs={{28,0},{29,1},{30,2},{31,3},{0,4},{1,5},{2,6},{3,7},{4,8},{5,9},{6... | collective-permute-start | bytes 786440 | tf_op jit(solution)/shard_map/ppermute | solution.py:184
  19.8 6.6 %back_4.1 = (f32[1024,512]{1,0:T(8,128)S(1)}, bf16[512,256]{1,0:T(8,128)(2,1)S(1)}, bf16[512,256]{1,0:T(8,128)(2,1)S(1)}) custom-call(s32[1]{0:T(128)} %bitcast.refs_0_, s32[1,512]{1,0:T(1,128)S(1)} %copy-done.5, s32[1,512]{1,0:T(1,128)S(1)} %copy-done.5, bf16[512,1024]{1,0:T(8,128)(2,1)S(1)} %bitcast.24, ...), custom_call_target="tpu_custom_call", output_to_operand_aliasing={{0}: (6, {})} | custom-call | flops 134217728 | bytes 1024 | tf_op jit(solution)/shard_map/back_4/pallas_call | solution.py:168
  26.5 5.7 %own_most.1 = (f32[1024,512]{1,0:T(8,128)S(1)}, f32[512,256]{1,0:T(8,128)S(1)}) custom-call(s32[1]{0:T(128)} %bitcast.refs_0_, s32[1,512]{1,0:T(1,128)S(1)} %copy-done.5, s32[1,512]{1,0:T(1,128)S(1)} %copy-done.5, bf16[512,1024]{1,0:T(8,128)(2,1)S(1)} %bitcast.25, bf16[512,1024]{1,0:T(8,128)(2,1)S(1)} %bitcast.18, ...), custom_call_target="tpu_custom_call", output_to_operand_aliasing={{0}: (7, {})} | custom-call | flops 80530640 | bytes 1024 | tf_op jit(solution)/shard_map/own_most/pallas_call | solution.py:168
  33.2 3.5 %collective-permute-start.8 = (bf16[1024,256]{1,0:T(8,128)(2,1)S(1)}, bf16[1024,256]{1,0:T(8,128)(2,1)S(1)}, u32[]{:S(2)}, u32[]{:S(2)}) collective-permute-start(bf16[1024,256]{1,0:T(8,128)(2,1)S(1)} %get-tuple-element.44), channel_id=1, source_target_pairs={{1,0},{2,1},{3,2},{4,3},{5,4},{6,5},{7,6},{8,7},{9,8},{10,9},{11,1... | collective-permute-start | bytes 1572872 | tf_op jit(solution)/shard_map/ppermute | solution.py:184
  36.7 6.7 %back_6_2.1 = (f32[1024,512]{1,0:T(8,128)S(1)}, bf16[1024,256]{1,0:T(8,128)(2,1)S(1)}) custom-call(s32[1]{0:T(128)} %bitcast.refs_0_, s32[1,512]{1,0:T(1,128)S(1)} %copy-done.5, s32[1,512]{1,0:T(1,128)S(1)} %copy-done.5, bf16[512,1024]{1,0:T(8,128)(2,1)S(1)} %bitcast.27, bf16[512,1024]{1,0:T(8,128)(2,1)S(1)} %bitcast.20, ...), custom_call_target="tpu_custom_call", output_to_operand_aliasing={{0}: (6, {})} | custom-call | flops 268435456 | bytes 1024 | tf_op jit(solution)/shard_map/back_6_2/pallas_call | solution.py:168
  43.4 2.7 %collective-permute-start.10 = (bf16[1024,256]{1,0:T(8,128)(2,1)S(1)}, bf16[1024,256]{1,0:T(8,128)(2,1)S(1)}, u32[]{:S(2)}, u32[]{:S(2)}) collective-permute-start(bf16[1024,256]{1,0:T(8,128)(2,1)S(1)} %get-tuple-element.47), channel_id=1, source_target_pairs={{2,0},{3,1},{4,2},{5,3},{6,4},{7,5},{8,6},{9,7},{10,8},{11,9},{12,... | collective-permute-start | bytes 1572872 | tf_op jit(solution)/shard_map/ppermute | solution.py:184
  46.0 6.5 %back_7_3.1 = (f32[1024,512]{1,0:T(8,128)S(1)}, bf16[512,256]{1,0:T(8,128)(2,1)S(1)}, bf16[512,256]{1,0:T(8,128)(2,1)S(1)}, bf16[512,768]{1,0:T(8,128)(2,1)S(1)}) custom-call(s32[1]{0:T(128)} %bitcast.refs_0_, s32[1,512]{1,0:T(1,128)S(1)} %copy-done.5, s32[1,512]{1,0:T(1,128)S(1)} %copy-done.5, ...), custom_call_target="tpu_custom_call", output_to_operand_aliasing={{0}: (6, {})} | custom-call | flops 268435456 | bytes 1024 | tf_op jit(solution)/shard_map/back_7_3/pallas_call | solution.py:168
  53.2 1.5 %collective-permute-start.11 = (bf16[512,256]{1,0:T(8,128)(2,1)S(1)}, bf16[512,256]{1,0:T(8,128)(2,1)S(1)}, u32[]{:S(2)}, u32[]{:S(2)}) collective-permute-start(bf16[512,256]{1,0:T(8,128)(2,1)S(1)} %get-tuple-element.48), channel_id=1, source_target_pairs={{7,0},{8,1},{9,2},{10,3},{11,4},{12,5},{13,6},{14,7},{15,8},{16,9}... | collective-permute-start | bytes 786440 | tf_op jit(solution)/shard_map/ppermute | solution.py:184
  54.7 6.0 %collective-permute-start.12 = (bf16[512,256]{1,0:T(8,128)(2,1)S(1)}, bf16[512,256]{1,0:T(8,128)(2,1)S(1)}, u32[]{:S(2)}, u32[]{:S(2)}) collective-permute-start(bf16[512,256]{1,0:T(8,128)(2,1)S(1)} %get-tuple-element.49), channel_id=1, source_target_pairs={{3,0},{4,1},{5,2},{6,3},{7,4},{8,5},{9,6},{10,7},{11,8},{12,9},{13... | collective-permute-start | bytes 786440 | tf_op jit(solution)/shard_map/ppermute | solution.py:184
  60.7 2.6 %own_last.1 = (bf16[512,256]{1,0:T(8,128)(2,1)S(1)}, f32[512,256]{1,0:T(8,128)S(1)}, f32[512,256]{1,0:T(8,128)S(1)}) custom-call(s32[1]{0:T(128)} %bitcast.refs_0_, s32[1,512]{1,0:T(1,128)S(1)} %copy-done.5, s32[1,512]{1,0:T(1,128)S(1)} %copy-done.5, bf16[512,1024]{1,0:T(8,128)(2,1)S(1)} %bitcast.29, bf16[512,1024]{1,0:T(8,128)(2,1)S(1)} %bitcast.22, ...), custom_call_target="tpu_custom_call" | custom-call | flops 53687092 | bytes 1024 | tf_op jit(solution)/shard_map/own_last/pallas_call | solution.py:168
  63.4 1.8 %collective-permute-start.13 = (bf16[512,256]{1,0:T(8,128)(2,1)S(1)}, bf16[512,256]{1,0:T(8,128)(2,1)S(1)}, u32[]{:S(2)}, u32[]{:S(2)}) collective-permute-start(bf16[512,256]{1,0:T(8,128)(2,1)S(1)} %add_convert_fusion), channel_id=1, source_target_pairs={{4,0},{5,1},{6,2},{7,3},{8,4},{9,5},{10,6},{11,7},{12,8},{13,9},{1... | collective-permute-start | bytes 786440 | tf_op jit(solution)/shard_map/ppermute | solution.py:184
  65.1 1.4 %collective-permute-start.9 = (bf16[512,256]{1,0:T(8,128)(2,1)S(1)}, bf16[512,256]{1,0:T(8,128)(2,1)S(1)}, u32[]{:S(2)}, u32[]{:S(2)}) collective-permute-start(bf16[512,256]{1,0:T(8,128)(2,1)S(1)} %get-tuple-element.45), channel_id=1, source_target_pairs={{32,0},{64,32},{96,64},{0,96},{33,1},{65,33},{97,65},{1,97},{34,2}... | collective-permute-start | bytes 786440 | tf_op jit(solution)/shard_map/ppermute | solution.py:184
  66.6 6.5 %collective-permute-done.11.rest_0_ = bf16[512,256]{1,0:T(8,128)(2,1)S(1)} collective-permute-done((bf16[512,256]{1,0:T(8,128)(2,1)S(1)}, bf16[512,256]{1,0:T(8,128)(2,1)S(1)}, u32[]{:S(2)}, u32[]{:S(2)}) %collective-permute-start.11) | collective-permute-done | bytes 262176 | tf_op jit(solution)/shard_map/ppermute | solution.py:184
  73.1 4.2 %collective-permute-done.12.rest_1_ = bf16[512,256]{1,0:T(8,128)(2,1)S(1)} collective-permute-done((bf16[512,256]{1,0:T(8,128)(2,1)S(1)}, bf16[512,256]{1,0:T(8,128)(2,1)S(1)}, u32[]{:S(2)}, u32[]{:S(2)}) %collective-permute-start.12) | collective-permute-done | bytes 262176 | tf_op jit(solution)/shard_map/ppermute | solution.py:184
  77.2 2.2 %collective-permute-done.13.rest_2_ = bf16[512,256]{1,0:T(8,128)(2,1)S(1)} collective-permute-done((bf16[512,256]{1,0:T(8,128)(2,1)S(1)}, bf16[512,256]{1,0:T(8,128)(2,1)S(1)}, u32[]{:S(2)}, u32[]{:S(2)}) %collective-permute-start.13) | collective-permute-done | bytes 262176 | tf_op jit(solution)/shard_map/ppermute | solution.py:184
  79.5 16.4 %collective-permute-done.7.rest_3_ = bf16[512,768]{1,0:T(8,128)(2,1)S(1)} collective-permute-done((bf16[512,768]{1,0:T(8,128)(2,1)S(1)}, bf16[512,768]{1,0:T(8,128)(2,1)S(1)}, u32[]{:S(2)}, u32[]{:S(2)}) %collective-permute-start.7) | collective-permute-done | bytes 786464 | tf_op jit(solution)/shard_map/ppermute | solution.py:184
  96.1 2.6 %collective-permute-done.9 = bf16[512,256]{1,0:T(8,128)(2,1)S(1)} collective-permute-done((bf16[512,256]{1,0:T(8,128)(2,1)S(1)}, bf16[512,256]{1,0:T(8,128)(2,1)S(1)}, u32[]{:S(2)}, u32[]{:S(2)}) %collective-permute-start.9) | collective-permute-done | bytes 262176 | tf_op jit(solution)/shard_map/ppermute | solution.py:184
  99.8 3.6 %collective-permute-done.14 = bf16[512,256]{1,0:T(8,128)(2,1)S(1)} collective-permute-done((bf16[512,256]{1,0:T(8,128)(2,1)S(1)}, bf16[512,256]{1,0:T(8,128)(2,1)S(1)}, u32[]{:S(2)}, u32[]{:S(2)}) %collective-permute-start.14) | collective-permute-done | bytes 262176 | tf_op jit(solution)/shard_map/ppermute | solution.py:184
  (33 shorter events, 7.1 us)
Async XLA Ops:
  0.6 9.9 %copy-start.5 = (s32[1,512]{1,0:T(1,128)S(1)}, s32[1,512]{1,0:T(1,128)}, u32[]{:S(2)}) copy-start(s32[1,512]{1,0:T(1,128)} %refs_2_.13) | copy-start | bytes 6148
  1.6 8.8 %collective-permute-start = (bf16[512,256]{1,0:T(8,128)(2,1)S(1)}, bf16[512,256]{1,0:T(8,128)(2,1)}, u32[]{:S(2)}, u32[]{:S(2)}) collective-permute-start(bf16[512,256]{1,0:T(8,128)(2,1)S(1)} %pad_maximum_fusion.kv_ref.refs_8_.refs_6_), channel_id=1, source_target_pairs={{31,0},{0,1},{1,2},{2,3},{3,4},{4,5},{5,6},{6,7},{7,8},{8,9},{9,10... | collective-permute-start | bytes 786440 | tf_op jit(solution)/shard_map/ppermute | solution.py:184
  1.7 18.1 %collective-permute-start.1 = (bf16[512,256]{1,0:T(8,128)(2,1)S(1)}, bf16[512,256]{1,0:T(8,128)(2,1)}, u32[]{:S(2)}, u32[]{:S(2)}) collective-permute-start(bf16[512,256]{1,0:T(8,128)(2,1)S(1)} %pad_maximum_fusion.kv_ref.refs_8_.refs_6_), channel_id=1, source_target_pairs={{28,0},{29,1},{30,2},{31,3},{0,4},{1,5},{2,6},{3,7},{4,8},{5,9},{6... | collective-permute-start | bytes 786440 | tf_op jit(solution)/shard_map/ppermute | solution.py:184
  2.3 1.2 %copy-start = (bf16[1,512,1024]{2,1,0:T(8,128)(2,1)S(1)}, bf16[1,512,1024]{2,1,0:T(8,128)(2,1)}, u32[]{:S(2)}) copy-start(bf16[1,512,1024]{2,1,0:T(8,128)(2,1)} %param.11) | copy-start | bytes 3145732
  3.6 1.2 %copy-start.3 = (bf16[1,512,1024]{2,1,0:T(8,128)(2,1)S(1)}, bf16[1,512,1024]{2,1,0:T(8,128)(2,1)}, u32[]{:S(2)}) copy-start(bf16[1,512,1024]{2,1,0:T(8,128)(2,1)} %param.10) | copy-start | bytes 3145732
  4.8 0.7 copy-start.4
  5.5 0.7 copy-start.6
  6.2 4.3 %copy-start.1 = (bf16[1,512,1024]{2,1,0:T(8,128)(2,1)S(1)}, bf16[1,512,1024]{2,1,0:T(8,128)(2,1)}, u32[]{:S(2)}) copy-start(bf16[1,512,1024]{2,1,0:T(8,128)(2,1)} %param.11) | copy-start | bytes 3145732
  8.2 11.6 %collective-permute-start.2 = (bf16[512,256]{1,0:T(8,128)(2,1)}, bf16[512,256]{1,0:T(8,128)(2,1)}, u32[]{:S(2)}, u32[]{:S(2)}) collective-permute-start(bf16[512,256]{1,0:T(8,128)(2,1)} %get-tuple-element.30), channel_id=1, source_target_pairs={{30,0},{31,1},{0,2},{1,3},{2,4},{3,5},{4,6},{5,7},{6,8},{7,9},{8,1... | collective-permute-start | bytes 786440 | tf_op jit(solution)/shard_map/ppermute | solution.py:184
  10.5 1.2 %copy-start.2 = (bf16[1,512,1024]{2,1,0:T(8,128)(2,1)S(1)}, bf16[1,512,1024]{2,1,0:T(8,128)(2,1)}, u32[]{:S(2)}) copy-start(bf16[1,512,1024]{2,1,0:T(8,128)(2,1)} %param.7) | copy-start | bytes 3145732
  18.3 13.9 %collective-permute-start.3 = (bf16[512,256]{1,0:T(8,128)(2,1)S(1)}, bf16[512,256]{1,0:T(8,128)(2,1)S(1)}, u32[]{:S(2)}, u32[]{:S(2)}) collective-permute-start(bf16[512,256]{1,0:T(8,128)(2,1)S(1)} %get-tuple-element.33), channel_id=1, source_target_pairs={{28,0},{29,1},{30,2},{31,3},{0,4},{1,5},{2,6},{3,7},{4,8},{5,9},{6... | collective-permute-start | bytes 786440 | tf_op jit(solution)/shard_map/ppermute | solution.py:184
  19.6 12.6 %collective-permute-start.4 = (bf16[512,256]{1,0:T(8,128)(2,1)S(1)}, bf16[512,256]{1,0:T(8,128)(2,1)S(1)}, u32[]{:S(2)}, u32[]{:S(2)}) collective-permute-start(bf16[512,256]{1,0:T(8,128)(2,1)S(1)} %get-tuple-element.35), channel_id=1, source_target_pairs={{29,0},{30,1},{31,2},{0,3},{1,4},{2,5},{3,6},{4,7},{5,8},{6,9},{7,... | collective-permute-start | bytes 786440 | tf_op jit(solution)/shard_map/ppermute | solution.py:184
  26.4 10.3 %collective-permute-start.5 = (bf16[512,256]{1,0:T(8,128)(2,1)S(1)}, bf16[512,256]{1,0:T(8,128)(2,1)S(1)}, u32[]{:S(2)}, u32[]{:S(2)}) collective-permute-start(bf16[512,256]{1,0:T(8,128)(2,1)S(1)} %get-tuple-element.37), channel_id=1, source_target_pairs={{28,0},{29,1},{30,2},{31,3},{0,4},{1,5},{2,6},{3,7},{4,8},{5,9},{6... | collective-permute-start | bytes 786440 | tf_op jit(solution)/shard_map/ppermute | solution.py:184
  32.9 13.1 %collective-permute-start.6 = (bf16[512,256]{1,0:T(8,128)(2,1)S(1)}, bf16[512,256]{1,0:T(8,128)(2,1)S(1)}, u32[]{:S(2)}, u32[]{:S(2)}) collective-permute-start(bf16[512,256]{1,0:T(8,128)(2,1)S(1)} %get-tuple-element.39), channel_id=1, source_target_pairs={{28,0},{29,1},{30,2},{31,3},{0,4},{1,5},{2,6},{3,7},{4,8},{5,9},{6... | collective-permute-start | bytes 786440 | tf_op jit(solution)/shard_map/ppermute | solution.py:184
  33.2 27.5 %collective-permute-start.8 = (bf16[1024,256]{1,0:T(8,128)(2,1)S(1)}, bf16[1024,256]{1,0:T(8,128)(2,1)S(1)}, u32[]{:S(2)}, u32[]{:S(2)}) collective-permute-start(bf16[1024,256]{1,0:T(8,128)(2,1)S(1)} %get-tuple-element.44), channel_id=1, source_target_pairs={{1,0},{2,1},{3,2},{4,3},{5,4},{6,5},{7,6},{8,7},{9,8},{10,9},{11,1... | collective-permute-start | bytes 1572872 | tf_op jit(solution)/shard_map/ppermute | solution.py:184
  43.4 19.9 %collective-permute-start.10 = (bf16[1024,256]{1,0:T(8,128)(2,1)S(1)}, bf16[1024,256]{1,0:T(8,128)(2,1)S(1)}, u32[]{:S(2)}, u32[]{:S(2)}) collective-permute-start(bf16[1024,256]{1,0:T(8,128)(2,1)S(1)} %get-tuple-element.47), channel_id=1, source_target_pairs={{2,0},{3,1},{4,2},{5,3},{6,4},{7,5},{8,6},{9,7},{10,8},{11,9},{12,... | collective-permute-start | bytes 1572872 | tf_op jit(solution)/shard_map/ppermute | solution.py:184
  52.6 43.2 %collective-permute-start.7 = (bf16[512,768]{1,0:T(8,128)(2,1)S(1)}, bf16[512,768]{1,0:T(8,128)(2,1)S(1)}, u32[]{:S(2)}, u32[]{:S(2)}) collective-permute-start(bf16[512,768]{1,0:T(8,128)(2,1)S(1)} %get-tuple-element.40), channel_id=1, source_target_pairs={{32,0},{64,32},{96,64},{0,96},{33,1},{65,33},{97,65},{1,97},{34,2}... | collective-permute-start | bytes 2359304 | tf_op jit(solution)/shard_map/ppermute | solution.py:184
  53.2 19.9 %collective-permute-start.11 = (bf16[512,256]{1,0:T(8,128)(2,1)S(1)}, bf16[512,256]{1,0:T(8,128)(2,1)S(1)}, u32[]{:S(2)}, u32[]{:S(2)}) collective-permute-start(bf16[512,256]{1,0:T(8,128)(2,1)S(1)} %get-tuple-element.48), channel_id=1, source_target_pairs={{7,0},{8,1},{9,2},{10,3},{11,4},{12,5},{13,6},{14,7},{15,8},{16,9}... | collective-permute-start | bytes 786440 | tf_op jit(solution)/shard_map/ppermute | solution.py:184
  54.7 22.5 %collective-permute-start.12 = (bf16[512,256]{1,0:T(8,128)(2,1)S(1)}, bf16[512,256]{1,0:T(8,128)(2,1)S(1)}, u32[]{:S(2)}, u32[]{:S(2)}) collective-permute-start(bf16[512,256]{1,0:T(8,128)(2,1)S(1)} %get-tuple-element.49), channel_id=1, source_target_pairs={{3,0},{4,1},{5,2},{6,3},{7,4},{8,5},{9,6},{10,7},{11,8},{12,9},{13... | collective-permute-start | bytes 786440 | tf_op jit(solution)/shard_map/ppermute | solution.py:184
  63.4 16.1 %collective-permute-start.13 = (bf16[512,256]{1,0:T(8,128)(2,1)S(1)}, bf16[512,256]{1,0:T(8,128)(2,1)S(1)}, u32[]{:S(2)}, u32[]{:S(2)}) collective-permute-start(bf16[512,256]{1,0:T(8,128)(2,1)S(1)} %add_convert_fusion), channel_id=1, source_target_pairs={{4,0},{5,1},{6,2},{7,3},{8,4},{9,5},{10,6},{11,7},{12,8},{13,9},{1... | collective-permute-start | bytes 786440 | tf_op jit(solution)/shard_map/ppermute | solution.py:184
  65.1 33.5 %collective-permute-start.9 = (bf16[512,256]{1,0:T(8,128)(2,1)S(1)}, bf16[512,256]{1,0:T(8,128)(2,1)S(1)}, u32[]{:S(2)}, u32[]{:S(2)}) collective-permute-start(bf16[512,256]{1,0:T(8,128)(2,1)S(1)} %get-tuple-element.45), channel_id=1, source_target_pairs={{32,0},{64,32},{96,64},{0,96},{33,1},{65,33},{97,65},{1,97},{34,2}... | collective-permute-start | bytes 786440 | tf_op jit(solution)/shard_map/ppermute | solution.py:184
  96.0 7.4 %collective-permute-start.14 = (bf16[512,256]{1,0:T(8,128)(2,1)S(1)}, bf16[512,256]{1,0:T(8,128)(2,1)S(1)}, u32[]{:S(2)}, u32[]{:S(2)}) collective-permute-start(bf16[512,256]{1,0:T(8,128)(2,1)S(1)} %sums.1), channel_id=1, source_target_pairs={{32,0},{64,32},{96,64},{0,96},{33,1},{65,33},{97,65},{1,97},{34,2}... | collective-permute-start | bytes 786440 | tf_op jit(solution)/shard_map/ppermute | solution.py:184
